TPU v7x, 128 devices: a whole 4x4x4 slice. The times are simulated.
128 devices in a mesh: seg: 16 (over y, x), blk: 8 (over z, core).
Axes of the slice: x: 4, y: 4, z: 4, core: 2. Of those that a mesh axis runs over, the one named last changes fastest.
Arguments:
- tokens: bfloat16 [128, 512, 768], P('seg', 'blk'), may hold values from -6 to 6
- memory: bfloat16 [128, 20, 768], P('seg'), may hold values from -6 to 6
- mem_init: bfloat16 [20, 768], replicated, may hold values from -6 to 6
- reset_flags: int32 [128], P('seg'), may hold values 0 or 1
- doc_ids: int32 [128, 512], P('seg'), may hold values from 0 to 2, as said below
- w_qkv: bfloat16 [768, 2304], replicated, may hold values from -0.21875 to 0.21875
- b_query: bfloat16 [768], replicated, may hold values from -3 to 3
- b_value: bfloat16 [768], replicated, may hold values from -3 to 3
- w_out: bfloat16 [768, 768], replicated, may hold values from -3.5 to 3.5
- b_out: bfloat16 [768], replicated, may hold values from -2 to 2
- norm1_gain: bfloat16 [768], replicated, may hold values from 0.099609375 to 1.8984375
- norm1_bias: bfloat16 [768], replicated, may hold values from -2 to 2
- w_in: bfloat16 [768, 3072], replicated, may hold values from -0.21875 to 0.21875
- b_in: bfloat16 [3072], replicated, may hold values from -3 to 3
- w_down: bfloat16 [3072, 768], replicated, may hold values from -0.109375 to 0.109375
- b_down: bfloat16 [768], replicated, may hold values from -2 to 2
- norm2_gain: bfloat16 [768], replicated, may hold values from 0.099609375 to 1.8984375
- norm2_bias: bfloat16 [768], replicated, may hold values from -2 to 2
- out_cot: bfloat16 [128, 512, 768], P('seg', 'blk'), may hold values from -6 to 6
- mem_cot: bfloat16 [128, 20, 768], P('seg'), may hold values from -6 to 6
Outputs:
- output: bfloat16 [128, 512, 768], P('seg', 'blk')
- mem_output: bfloat16 [128, 20, 768], P('seg')
- grad_tokens: bfloat16 [128, 512, 768], P('seg', 'blk')
- grad_memory: bfloat16 [128, 20, 768], P('seg')
- grad_mem_init: float32 [20, 768], replicated
- grad_w_qkv: float32 [768, 2304], replicated
- grad_b_query: float32 [768], replicated
- grad_b_value: float32 [768], replicated
- grad_w_out: float32 [768, 768], replicated
- grad_b_out: float32 [768], replicated
- grad_norm1_gain: float32 [768], replicated
- grad_norm1_bias: float32 [768], replicated
- grad_w_in: float32 [768, 3072], replicated
- grad_b_in: float32 [3072], replicated
- grad_w_down: float32 [3072, 768], replicated
- grad_b_down: float32 [768], replicated
- grad_norm2_gain: float32 [768], replicated
- grad_norm2_bias: float32 [768], replicated
Inputs may be any that keep to these rules, and one draw needn't show every extreme that they name: `doc_ids`: within a segment the numbers never fall and take the values 0, 1 and 2; document 1 starts before position 64 and ends at or after position 448.
All inputs are finite; a program needn't handle non-finite values. No bound on the sum of `reset_flags` on one device may be relied on, other than what follows from the above.
Results may differ from a plain program's by a relative error of at most 0.028.
Values may be sent and summed in bfloat16 or wider, within the bound.
No kernel may reach another device: no remote copies, remote signals or barrier semaphores. Data moves between devices by JAX's collectives and lax.ppermute only.
A program may use at most 256 MiB of HBM per device.

v0:
```python
import jax
import jax.numpy as jnp
from jax import lax
from jax.experimental import pallas as pl
from jax.experimental.pallas import tpu as pltpu
from jax.sharding import Mesh, PartitionSpec as P

F32 = jnp.float32
BF16 = jnp.bfloat16
HEADS = 12
EPS = 1e-12
BAN = 2.0**30
VMEM_ASK = 60 * 1024 * 1024
BLK = ("z", "core")
SEG = ("y", "x")
ALL = ("y", "x", "z", "core")
XYZ = ("x", "y", "z")
CHIPS = 64
ROW_PAD = 12
SPARE_ROWS = 256


def dot(left, right):
    return jnp.dot(left, right, preferred_element_type=F32)


def dot_nt(left, right):
    return lax.dot_general(left, right, (((1,), (1,)), ((), ())), preferred_element_type=F32)


def dot_tn(left, right):
    return lax.dot_general(left, right, (((0,), (0,)), ((), ())), preferred_element_type=F32)


def cost(micros):
    return pl.CostEstimate(flops=int(micros * 1e9), bytes_accessed=0, transcendentals=0)


def lanes_of(shape):
    return lax.broadcasted_iota(jnp.int32, shape, 1)


def split_three(value):
    high = value.astype(BF16)
    rest = value - high.astype(F32)
    middle = rest.astype(BF16)
    low = (rest - middle.astype(F32)).astype(BF16)
    return high, middle, low


def norm_parts(value):
    centre = jnp.mean(value, axis=-1, keepdims=True)
    centered = value - centre
    spread = jnp.mean(centered * centered, axis=-1, keepdims=True)
    scale = lax.rsqrt(spread + EPS)
    return centered * scale, scale


def norm_back(grad, normal, scale):
    mean_grad = jnp.mean(grad, axis=-1, keepdims=True)
    mean_prod = jnp.mean(grad * normal, axis=-1, keepdims=True)
    return scale * (grad - mean_grad - normal * mean_prod)


def pack_rows(out, value, split, base=0):
    blocks = out.shape[0]
    each = split // blocks
    rest = value.shape[0] - split
    for block in range(blocks):
        out[block, base : base + each] = value[block * each : (block + 1) * each]
        out[block, base + each : base + each + rest] = value[split:]


def column_sum(value):
    return jnp.sum(value, axis=0, keepdims=True)


def attend_kernel(text, mem, w_q, w_k, w_v, lines, lines_all, mark_q, mark_k, w_out,
                  q_out, k_out, v_out, att_out, log_out, resid):
    step = pl.program_id(0)
    x = jnp.concatenate([text[...], mem[...]], axis=0)
    count = x.shape[0]
    query = (dot(x, w_q[...]) + lines[0:1, :]).astype(BF16)
    key = dot(x, w_k[...]).astype(BF16)
    value = (dot(x, w_v[...]) + lines[1:2, :]).astype(BF16)
    q_out[...] = query
    k_out[...] = key
    v_out[...] = value
    scaled = query * jnp.asarray(0.125, BF16)
    lane = lanes_of((count, 128))
    ones = (lane == 0).astype(BF16)
    mq, mk = mark_q[...], mark_k[...]
    logs = jnp.zeros((count, 128), F32)
    scores = []
    for head in range(4):
        span = slice(128 * (head // 2), 128 * (head // 2) + 128)
        mine = jnp.where(lane // 64 == head % 2, scaled[:, span], jnp.asarray(0, BF16))
        key_wide = jnp.concatenate([key[:, span], mk], axis=1)
        scores.append(dot_nt(jnp.concatenate([mine, mq], axis=1), key_wide))
    outs = []
    for head in range(4):
        span = slice(128 * (head // 2), 128 * (head // 2) + 128)
        value_wide = jnp.concatenate([value[:, span], ones], axis=1)
        top = jnp.max(scores[head], axis=-1, keepdims=True)
        raised = jnp.exp(scores[head] - top).astype(BF16)
        summed = dot(raised, value_wide)
        total = summed[:, 128:129]
        outs.append(summed[:, :128] / total)
        logs = jnp.where(lane == 4 * step + head, top + jnp.log(total), logs)
    pairs = [jnp.where(lane < 64, outs[0], outs[1]), jnp.where(lane < 64, outs[2], outs[3])]
    pairs = [pair.astype(BF16) for pair in pairs]
    attended = jnp.concatenate(pairs, axis=1)
    att_out[...] = attended

    @pl.when(step == 0)
    def _():
        log_out[...] = logs
        resid[...] = x.astype(F32) + lines_all[2:3, :]

    @pl.when(step > 0)
    def _():
        log_out[...] += logs

    resid[...] += dot(attended, w_out[...])


def attend(text, mem, w_qkv, lines, mark_q, mark_k, w_out):
    width = text.shape[1]
    count = text.shape[0] + mem.shape[0]
    whole = lambda shape: pl.BlockSpec(shape, lambda j: (0, 0))
    cols = lambda height, base: pl.BlockSpec((height, 256), lambda j: (0, base + j))
    low = jax.ShapeDtypeStruct((count, width), BF16)
    return pl.pallas_call(
        attend_kernel,
        grid=(3,),
        in_specs=[
            whole(text.shape),
            whole(mem.shape),
            cols(width, 0),
            cols(width, 3),
            cols(width, 6),
            cols(16, 0),
            whole((16, width)),
            whole((count, 128)),
            whole((count, 128)),
            pl.BlockSpec((256, width), lambda j: (j, 0)),
        ],
        out_specs=[
            cols(count, 0),
            cols(count, 0),
            cols(count, 0),
            cols(count, 0),
            whole((count, 128)),
            whole((count, width)),
        ],
        out_shape=[
            low,
            low,
            low,
            low,
            jax.ShapeDtypeStruct((count, 128), F32),
            jax.ShapeDtypeStruct((count, width), F32),
        ],
        compiler_params=pltpu.CompilerParams(vmem_limit_bytes=VMEM_ASK),
        cost_estimate=cost(15),
        name="attend",
    )(text, mem, w_qkv, w_qkv, w_qkv, lines, lines, mark_q, mark_k, w_out)


def feed_kernel(resid, lines, w_in, w_down, cot_text, cot_mem,
                result_out, g_two, inner_out, sums_out, sums_in_out, grad_down_out, grad_in_out,
                hidden_low, hidden_turned, g_low, act_all, slope_all):
    step = pl.program_id(0)
    half = pl.num_programs(0) // 2
    width = resid.shape[1]
    cuts = w_in.shape[1] // width

    @pl.when(step == 0)
    def _():
        normal, _ = norm_parts(resid[...])
        hidden = normal * lines[3:4, :] + lines[4:5, :]
        hidden_low[...] = hidden.astype(BF16)
        hidden_turned[...] = hidden.astype(BF16).T
        g_two[...] = hidden + lines[5:6, :]

    @pl.when(step < half)
    def _():
        spans = [slice(cut * width, (cut + 1) * width) for cut in range(cuts)]
        inners = [
            dot(hidden_low[...], w_in[:, spans[cut]]) + lines[pl.ds(8 + step * cuts + cut, 1), :]
            for cut in range(cuts)
        ]
        total = g_two[...]
        for cut, inner in enumerate(inners):
            part = step * cuts + cut
            phi = 0.5 * (1.0 + lax.erf(inner * (0.5**0.5)))
            act = (inner * phi).astype(BF16)
            act_all[part] = act
            slope = phi + inner * jnp.exp(-0.5 * inner * inner) * 0.3989422804014327
            slope_all[part] = slope.astype(BF16)
            total += dot(act, w_down[spans[cut], :])
        g_two[...] = total

    @pl.when(step == half - 1)
    def _():
        normal, scale = norm_parts(g_two[...])
        result = normal * lines[6:7, :] + lines[7:8, :]
        pack_rows(result_out, result.astype(BF16), cot_text.shape[0])
        grad = jnp.concatenate([cot_text[...], cot_mem[...]], axis=0).astype(F32)
        sums_out[0:1, :] = column_sum(grad * normal)
        sums_out[1:2, :] = column_sum(grad)
        grad = norm_back(grad * lines[6:7, :], normal, scale)
        sums_out[2:3, :] = column_sum(grad)
        g_two[...] = grad
        g_low[...] = grad.astype(BF16)

    @pl.when(step >= half)
    def _():
        spans = [slice(cut * width, (cut + 1) * width) for cut in range(cuts)]
        g_acts = [dot_nt(g_low[...], w_down[span, :]) for span in spans]
        for cut, span in enumerate(spans):
            part = (step - half) * cuts + cut
            grad_down_out[span, :] = dot_tn(act_all[part], g_low[...]).astype(BF16)
            g_inner = g_acts[cut] * slope_all[part].astype(F32)
            sums_in_out[0:1, span] = column_sum(g_inner)
            g_inner_low = g_inner.astype(BF16)
            inner_out[:, span] = g_inner_low
            grad_in_out[cut] = dot(hidden_turned[...], g_inner_low).astype(BF16)


def feed(resid, lines, w_in, w_down, cot_text, cot_mem, packed):
    count, width = resid.shape
    wide = w_in.shape[1]
    parts, cuts = wide // width, 2
    half = parts // cuts
    chunk = cuts * width
    whole = lambda shape: pl.BlockSpec(shape, lambda j: (0,) * len(shape))
    late = lambda j: jnp.maximum(j - half, 0)
    full = whole((count, width))
    high = jax.ShapeDtypeStruct((count, width), F32)
    return pl.pallas_call(
        feed_kernel,
        grid=(2 * half,),
        in_specs=[
            full,
            whole(lines.shape),
            pl.BlockSpec((width, chunk), lambda j: (0, jnp.minimum(j, half - 1))),
            pl.BlockSpec((chunk, width), lambda j: (j % half, 0)),
            whole(cot_text.shape),
            whole(cot_mem.shape),
        ],
        out_specs=[
            whole(packed),
            full,
            pl.BlockSpec((count, chunk), lambda j: (0, late(j))),
            whole((8, width)),
            pl.BlockSpec((8, chunk), lambda j: (0, late(j))),
            pl.BlockSpec((chunk, width), lambda j: (late(j), 0)),
            pl.BlockSpec((cuts, width, width), lambda j: (late(j), 0, 0)),
        ],
        out_shape=[
            jax.ShapeDtypeStruct(packed, BF16),
            high,
            jax.ShapeDtypeStruct((count, wide), BF16),
            jax.ShapeDtypeStruct((8, width), F32),
            jax.ShapeDtypeStruct((8, wide), F32),
            jax.ShapeDtypeStruct((wide, width), BF16),
            jax.ShapeDtypeStruct((parts, width, width), BF16),
        ],
        scratch_shapes=[
            pltpu.VMEM((count, width), BF16),
            pltpu.VMEM((width, count), BF16),
            pltpu.VMEM((count, width), BF16),
            pltpu.VMEM((parts, count, width), BF16),
            pltpu.VMEM((parts, count, width), BF16),
        ],
        compiler_params=pltpu.CompilerParams(vmem_limit_bytes=VMEM_ASK),
        cost_estimate=cost(28),
        name="feed",
    )(resid, lines, w_in, w_down, cot_text, cot_mem)


def backward_kernel(g_two, g_inner, w_in, resid, lines, text, mem, q, k, v, att, logs, mark_q, mark_k,
                    w_out, w_q, w_k, w_v, sums_two, sums_in, scalars, result,
                    mine_out, theirs_out, packed_out, g_rows, g_low, rows_turned, sums,
                    grads, sems):
    step = pl.program_id(0)
    parts = pl.num_programs(0) - 3

    @pl.when(step == 0)
    def _():
        x = jnp.concatenate([text[...], mem[...]], axis=0)
        rows_turned[...] = x.T
        g_rows[...] = g_two[...]
        packed_out[:, : result.shape[1]] = result[...]

    @pl.when(step < parts)
    def _():
        g_rows[...] += dot_nt(g_inner[...], w_in[...])

    @pl.when(step == parts - 1)
    def _():
        normal, scale = norm_parts(resid[...])
        g_hidden = g_rows[...]
        first = sums.shape[0] - 12
        sums[first + 2 : first + 3, :] = column_sum(g_hidden * normal)
        sums[first + 3 : first + 4, :] = column_sum(g_hidden)
        grad = norm_back(g_hidden * lines[3:4, :], normal, scale)
        sums[first + 4 : first + 5, :] = column_sum(grad)
        g_rows[...] = grad
        g_low[...] = grad.astype(BF16)

    @pl.when(step >= parts)
    def _():
        attend_back_step(step - parts, text, mem, q, k, v, att, logs, mark_q, mark_k, g_low, w_out,
                         w_q, w_k, w_v, sums_two, sums_in, scalars,
                         mine_out, theirs_out, packed_out, g_rows, rows_turned, sums,
                         grads, sems)


def attend_back_step(step, text, mem, q, k, v, att, logs, mark_q, mark_k, g_low, w_out,
                     w_q, w_k, w_v, sums_two, sums_in, scalars,
                     mine_out, theirs_out, packed_out, g_rows, rows_turned, sums,
                         grads, sems):
    core = scalars[0, 1]
    split = text.shape[0]
    count = split + mem.shape[0]
    width = text.shape[1]
    query, key, value, attended = q[...], k[...], v[...], att[...]

    def put(half, start, part):
        rows = pl.ds(pl.multiple_of(start, 16), part.shape[0])
        grads[jnp.where(core == half, 0, 1), rows, :] = part

    blocks = width // 128
    group_rows = grads.shape[1] // 2
    piece_rows = group_rows // 2

    def start_of(group, block):
        piece = block // (blocks // 2)
        return group * group_rows + piece * piece_rows + block % (blocks // 2) * width

    grad_w_out = dot_tn(attended, g_low[...]).astype(BF16)
    for block in range(blocks):
        part = grad_w_out[:, 128 * block : 128 * block + 128]
        put(1, start_of(1, block) + 256 * step, part)
    g_att = dot_nt(g_low[...], w_out[...])
    g_att_low = g_att.astype(BF16)
    scaled = query * jnp.asarray(0.125, BF16)
    product = g_att_low.astype(F32) * attended.astype(F32)
    lane = lanes_of((count, 128))
    none = jnp.asarray(0, BF16)
    thirds = ((lane >= 4) & (lane < 7)).astype(BF16)
    mq, mk = mark_q[...], mark_k[...] + thirds
    log_all = logs[...]

    def extra(column, base):
        high, middle, low = split_three(-column)
        wide = jnp.where(lane == 4, high, jnp.where(lane == 5, middle, low))
        return jnp.where((lane >= 4) & (lane < 7), wide, base)

    g_querys, g_keys, g_values = [], [], []
    for pair in range(2):
        span = slice(128 * pair, 128 * pair + 128)
        key_pair = key[:, span]
        key_wide = jnp.concatenate([key_pair, mk], axis=1)
        value_wide = jnp.concatenate([value[:, span], thirds], axis=1)
        key_turned = key_pair.astype(F32).T
        turned = lax.broadcasted_iota(jnp.int32, key_turned.shape, 0)
        g_query = g_key = g_value = None
        for side in range(2):
            own = lane // 64 == side
            mine = jnp.where(own, scaled[:, span], none)
            head = 4 * step + 2 * pair + side
            log_own = jnp.sum(jnp.where(lane == head, log_all, 0.0), axis=1, keepdims=True)
            query_wide = jnp.concatenate([mine, extra(log_own, mq)], axis=1)
            probs = jnp.exp(dot_nt(key_wide, query_wide))
            g_mine = jnp.where(own, g_att_low[:, span], none)
            delta = jnp.sum(jnp.where(own, product[:, span], 0.0), axis=1, keepdims=True)
            g_wide = jnp.concatenate([g_mine, extra(delta, jnp.zeros_like(mq))], axis=1)
            g_scores = (probs * dot_nt(value_wide, g_wide)).astype(BF16)
            part_v = dot(probs.astype(BF16), g_mine)
            part_k = dot(g_scores, mine)
            turned_own = jnp.where(turned // 64 == side, key_turned, 0.0).astype(BF16)
            part_q = dot(turned_own, g_scores)
            if side == 0:
                g_query, g_key, g_value = part_q, part_k, part_v
            else:
                g_query, g_key, g_value = g_query + part_q, g_key + part_k, g_value + part_v
        g_querys.append(g_query.T * 0.125)
        g_keys.append(g_key)
        g_values.append(g_value)
    g_query = jnp.concatenate(g_querys, axis=1)
    g_key = jnp.concatenate(g_keys, axis=1)
    g_value = jnp.concatenate(g_values, axis=1)
    columns = pl.ds(pl.multiple_of(256 * step, 256), 256)
    first = sums.shape[0] - 12
    sums[first : first + 1, columns] = column_sum(g_query)
    sums[first + 1 : first + 2, columns] = column_sum(g_value)
    total = g_rows[...]
    for place, (grad, weight) in enumerate(((g_query, w_q), (g_key, w_k), (g_value, w_v))):
        low = grad.astype(BF16)
        grad_w = dot(rows_turned[...], low).astype(BF16)
        for block in range(2):
            part = grad_w[:, 128 * block : 128 * block + 128]
            put(place // 2, start_of(place % 2, 2 * step + block), part)
        total += dot_nt(low, weight[...])
    g_rows[...] = total

    @pl.when(step == 2)
    def _():
        reset = scalars[0, 0] == 1
        g_mem = total[split:]
        zero = jnp.zeros_like(g_mem)
        g_kept = jnp.where(reset, zero, g_mem)
        g_all = jnp.concatenate([total[:split], g_kept], axis=0).astype(BF16)
        pack_rows(packed_out, g_all, split, packed_out.shape[1] // 2)
        first = sums.shape[0] - 12
        sums[first + 5 : first + 8, :] = sums_two[0:3, :]
        for place in range(4):
            sums[first + 8 + place : first + 9 + place, :] = sums_in[0:1, place * width : (place + 1) * width]
        mem_count = sums.shape[0] - 12
        sums[0:mem_count, :] = jnp.where(reset, g_mem, zero)[0:mem_count]
        small = sums[...].astype(BF16)
        base = blocks // 2 * width
        empty = jnp.zeros((SPARE_ROWS, 128), BF16)
        for place in range(4):
            rows = slice(place * piece_rows + base, (place + 1) * piece_rows)
            grads[0, rows, :] = empty
            grads[1, rows, :] = empty
        for place in range(2):
            for block in range(blocks):
                start = place * piece_rows + base + block * small.shape[0]
                put(0, start, small[:, 128 * block : 128 * block + 128])
        theirs = pltpu.make_async_copy(grads.at[1], theirs_out, sems.at[1])
        mine = pltpu.make_async_copy(grads.at[0], mine_out, sems.at[0])
        theirs.start()
        mine.start()
        theirs.wait()
        mine.wait()


def backward(g_two, g_inner, w_in, resid, lines, text, mem, q, k, v, att, logs, mark_q, mark_k,
             w_out, w_qkv, sums_two, sums_in, scalars, result):
    width = text.shape[1]
    count = text.shape[0] + mem.shape[0]
    chunk = 2 * width
    parts = w_in.shape[1] // chunk
    whole = lambda shape: pl.BlockSpec(shape, lambda j: (0,) * len(shape))
    early = lambda height: pl.BlockSpec((height, chunk), lambda j: (0, jnp.minimum(j, parts - 1)))
    quad = lambda j: jnp.maximum(j - parts, 0)
    cols = lambda height, base: pl.BlockSpec((height, 256), lambda j: (0, base + quad(j)))
    full = whole((count, width))
    mark = whole((count, 128))
    height = 2 * (width // 128 * width + 2 * SPARE_ROWS)
    half = jax.ShapeDtypeStruct((height, 128), BF16)
    packed = (result.shape[0], 2 * result.shape[1], width)
    return pl.pallas_call(
        backward_kernel,
        grid=(parts + 3,),
        in_specs=[
            full,
            early(count),
            early(width),
            full,
            whole(lines.shape),
            whole(text.shape),
            whole(mem.shape),
            cols(count, 0),
            cols(count, 0),
            cols(count, 0),
            cols(count, 0),
            mark,
            mark,
            mark,
            pl.BlockSpec((256, width), lambda j: (quad(j), 0)),
            cols(width, 0),
            cols(width, 3),
            cols(width, 6),
            whole(sums_two.shape),
            whole(sums_in.shape),
            pl.BlockSpec(memory_space=pltpu.SMEM),
            whole(result.shape),
        ],
        out_specs=[pl.BlockSpec(memory_space=pl.ANY)] * 2 + [whole(packed)],
        out_shape=[half, half, jax.ShapeDtypeStruct(packed, BF16)],
        scratch_shapes=[
            pltpu.VMEM((count, width), F32),
            pltpu.VMEM((count, width), BF16),
            pltpu.VMEM((width, count), BF16),
            pltpu.VMEM((count - text.shape[0] - ROW_PAD + 12, width), F32),
            pltpu.VMEM((2, height, 128), BF16),
            pltpu.SemaphoreType.DMA((2,)),
        ],
        compiler_params=pltpu.CompilerParams(vmem_limit_bytes=VMEM_ASK),
        cost_estimate=cost(33),
        name="backward",
    )(g_two, g_inner, w_in, resid, lines, text, mem, q, k, v, att, logs, mark_q, mark_k,
      w_out, w_qkv, w_qkv, w_qkv, sums_two, sums_in, scalars, result)


def widen_kernel(*refs):
    pieces, codes = refs[:4], refs[4]
    early = len(refs) == 10
    if early:
        qkv_out, out_out, small_out, wide, sems = refs[5:]
    else:
        qkv_out, out_out, wide, sems = refs[-4:]
    width = wide.shape[1]
    part = wide.shape[2]
    blocks = part // 128

    def copies(place):
        code = codes[0, place]
        in_qkv = code < 6
        spot = jnp.where(in_qkv, code, code - 6)
        columns = pl.ds(pl.multiple_of(spot * part, part), part)
        to_qkv = pltpu.make_async_copy(wide.at[place], qkv_out.at[:, columns], sems.at[place])
        to_out = pltpu.make_async_copy(wide.at[place], out_out.at[:, columns], sems.at[place])
        return in_qkv, to_qkv, to_out

    for place, piece in enumerate(pieces):
        for block in range(blocks):
            rows = slice(block * width, (block + 1) * width)
            wide[place, :, 128 * block : 128 * block + 128] = piece[rows, :].astype(F32)
        in_qkv, to_qkv, to_out = copies(place)

        if early:

            @pl.when(codes[0, place] < 2)
            def _():
                height = small_out.shape[0]
                for block in range(2 * blocks):
                    start = blocks * width + block * height
                    rows = piece[start : start + height, :].astype(F32)
                    small_out[:, 128 * block : 128 * block + 128] = rows

        @pl.when(in_qkv)
        def _():
            to_qkv.start()

        @pl.when(jnp.logical_not(in_qkv))
        def _():
            to_out.start()

    for place in range(4):
        in_qkv, to_qkv, to_out = copies(place)

        @pl.when(in_qkv)
        def _():
            to_qkv.wait()

        @pl.when(jnp.logical_not(in_qkv))
        def _():
            to_out.wait()


def widen(pieces, codes, width, small_count, partly=()):
    vmem = pl.BlockSpec(memory_space=pltpu.VMEM)
    hbm = pl.BlockSpec(memory_space=pl.ANY)
    return pl.pallas_call(
        widen_kernel,
        in_specs=[vmem] * 4 + [pl.BlockSpec(memory_space=pltpu.SMEM)] + [hbm] * len(partly),
        out_specs=[hbm, hbm] + ([] if partly else [vmem]),
        out_shape=[
            jax.ShapeDtypeStruct((width, 3 * width), F32),
            jax.ShapeDtypeStruct((width, width), F32),
        ]
        + ([] if partly else [jax.ShapeDtypeStruct((small_count, width), F32)]),
        scratch_shapes=[pltpu.VMEM((4, width, width // 2), F32), pltpu.SemaphoreType.DMA((4,))],
        input_output_aliases={5: 0, 6: 1} if partly else {},
        compiler_params=pltpu.CompilerParams(vmem_limit_bytes=VMEM_ASK),
        cost_estimate=cost(4),
        name="widen",
    )(*pieces, codes, *partly)


def widen_feed_kernel(down, inward, down_out, in_out, low, high, in_sems, out_sems):
    count, width = inward.shape[0], inward.shape[2]
    low_rows = low.shape[1]
    cut = width // low_rows
    places = []
    for part in range(count):
        for piece in range(cut):
            rows = pl.ds(piece * low_rows, low_rows)
            tall = pl.ds(part * width + piece * low_rows, low_rows)
            columns = pl.ds(part * width, width)
            places.append((inward.at[part, rows], in_out.at[rows, columns]))
            places.append((down.at[tall], down_out.at[tall]))
    fetches, sends = [], []
    for place, (source, target) in enumerate(places):
        fetches.append(pltpu.make_async_copy(source, low.at[place], in_sems.at[place]))
        sends.append(pltpu.make_async_copy(high.at[place], target, out_sems.at[place]))
        fetches[-1].start()
    for place in range(len(places)):
        fetches[place].wait()
        high[place] = low[place].astype(F32)
        sends[place].start()
    for send in sends:
        send.wait()


def widen_feed(down, inward):
    count, height, width = inward.shape
    cut = 2
    blocks = 2 * count * cut
    hbm = pl.BlockSpec(memory_space=pl.ANY)
    return pl.pallas_call(
        widen_feed_kernel,
        in_specs=[hbm, hbm],
        out_specs=[hbm, hbm],
        out_shape=[
            jax.ShapeDtypeStruct(down.shape, F32),
            jax.ShapeDtypeStruct((height, count * width), F32),
        ],
        scratch_shapes=[
            pltpu.VMEM((blocks, height // cut, width), BF16),
            pltpu.VMEM((blocks, height // cut, width), F32),
            pltpu.SemaphoreType.DMA((blocks,)),
            pltpu.SemaphoreType.DMA((blocks,)),
        ],
        compiler_params=pltpu.CompilerParams(vmem_limit_bytes=VMEM_ASK),
        cost_estimate=cost(9),
        name="widen_feed",
    )(down, inward)


def ring_partner(place, way):
    return place ^ 1 if way == 0 else 3 - place


def ring_pairs(step):
    pairs = []
    for place in range(4):
        for core in range(2):
            other = ring_partner(place, (step + core) % 2)
            pairs.append((2 * place + core, 2 * other + core))
    return pairs


def side_of(place, core, step):
    return jnp.where((step + core) % 2 == 0, (place + 1) // 2 % 2, place // 2)


def ring_side(axis, step):
    return side_of(lax.axis_index(axis), lax.axis_index("core"), step)


def ring_swap(value, axis, step):
    return lax.ppermute(value, (axis, "core"), ring_pairs(step))


def core_swap(value):
    return lax.ppermute(value, "core", [(0, 1), (1, 0)])


def add_pair(pair):
    return (pair[0].astype(F32) + pair[1].astype(F32)).astype(BF16)


def half_of(pair, side, start=0, rows=None):
    rows = pair[0].shape[-2] if rows is None else rows
    axis = pair[0].ndim - 2
    place = start + side * (rows // 2)
    return add_pair([lax.dynamic_slice_in_dim(part, place, rows // 2, axis) for part in pair])


def ring_halve(pair, axis, step, start=0, rows=None):
    side = ring_side(axis, step)
    got = ring_swap(half_of(pair, 1 - side, start, rows), axis, step)
    return half_of(pair, side, start, rows), got


def ring_join(value, axis, step):
    got = ring_swap(value, axis, step)
    return jnp.where(
        ring_side(axis, step) == 0,
        jnp.concatenate([value, got], axis=-2),
        jnp.concatenate([got, value], axis=-2),
    )


def to_segments(value):
    return lax.all_to_all(value, BLK, 0, 1, tiled=True)[0]


def after(value, other):
    return lax.optimization_barrier((value, other))[0]


def doc_marks(docs, mem_count):
    kinds = (docs[:, None] == jnp.arange(3)[None]).astype(F32)
    rest = mem_count + ROW_PAD
    total = docs.shape[0] + rest
    spare = (jnp.arange(total) >= total - ROW_PAD).astype(F32)[:, None]
    query = jnp.concatenate([jnp.pad(kinds, ((0, rest), (0, 0))), jnp.ones((total, 1), F32)], 1)
    key = jnp.concatenate([jnp.pad(kinds - 1.0, ((0, rest), (0, 0))), -spare], 1) * BAN
    fill = ((0, 0), (0, 128 - query.shape[1]))
    return jnp.pad(query, fill).astype(BF16), jnp.pad(key, fill).astype(BF16)


def local(
    tokens,
    memory,
    mem_init,
    reset_flags,
    doc_ids,
    w_qkv,
    b_query,
    b_value,
    w_out,
    b_out,
    norm1_gain,
    norm1_bias,
    w_in,
    b_in,
    w_down,
    b_down,
    norm2_gain,
    norm2_bias,
    out_cot,
    mem_cot,
):
    seg_count, tok_count, width = tokens.shape
    mem_count = memory.shape[1]
    place = lax.axis_index(BLK)
    pick = lambda value: lax.dynamic_index_in_dim(value, place, 0, keepdims=False)
    fill = lambda value: jnp.pad(value, ((0, ROW_PAD), (0, 0)))
    packed = (seg_count, tok_count + mem_count + ROW_PAD, width)
    my_flag = pick(reset_flags)
    mark_q, mark_k = doc_marks(pick(doc_ids), mem_count)
    mem = fill(jnp.where(my_flag == 1, mem_init, pick(memory)))
    cot_mem = fill(pick(mem_cot))
    text = to_segments(tokens)
    cot_text = to_segments(after(out_cot, text))

    lines = jnp.concatenate(
        [b_query, b_value, b_out, norm1_gain, norm1_bias, b_down, norm2_gain, norm2_bias, b_in]
    )
    lines = jnp.pad(lines.astype(F32).reshape(-1, width), ((0, 4), (0, 0)))
    q, k, v, att, logs, resid = attend(text, mem, w_qkv, lines, mark_q, mark_k, w_out)
    result, g_two, g_inner, sums_two, sums_in, grad_down, grad_in = feed(
        resid, lines, w_in, w_down, cot_text, cot_mem, packed
    )
    grad_down, grad_in = lax.psum((grad_down, grad_in), ALL)
    scalars = jnp.stack([my_flag, lax.axis_index("core")]).reshape(1, 2).astype(jnp.int32)
    small_count = mem_count + 12

    def attention_back(operands):
        result, g_two, g_inner, sums_two, sums_in = operands
        mine, theirs, g_packed = backward(
            g_two,
            g_inner,
            w_in,
            resid,
            lines,
            text,
            mem,
            q,
            k,
            v,
            att,
            logs,
            mark_q,
            mark_k,
            w_out,
            w_qkv,
            sums_two,
            sums_in,
            scalars,
            result,
        )
        pair = (mine, core_swap(theirs))
        rows = mine.shape[0] // 2
        over_z = ring_halve(pair, "z", 0, 0, rows)
        over_x = ring_halve(pair, "x", 0, rows, rows)
        over_z = ring_halve(over_z, "z", 1)
        over_x = ring_halve(over_x, "x", 1)
        both = lax.all_to_all(after(g_packed, over_z[0]), BLK, 0, 0, tiled=True)
        side = ring_side("y", 0)
        got = ring_swap(jnp.stack([half_of(over_z, 1 - side), half_of(over_x, 1 - side)]), "y", 0)
        pair = (jnp.stack([half_of(over_z, side), half_of(over_x, side)]), got)
        pair = ring_halve(pair, "y", 1)
        over_z, over_x = add_pair([part[0] for part in pair]), add_pair([part[1] for part in pair])
        for step in (0, 1):
            got_z, got_x = ring_swap(over_z, "x", step), ring_swap(over_x, "z", step)
            over_z, over_x = add_pair((over_z, got_z)), add_pair((over_x, got_x))
        joined = after(jnp.stack([over_z, over_x]), both)
        for step in (1, 0):
            joined = ring_join(joined, "y", step)
        over_z = ring_join(joined[0], "z", 1)
        over_x = ring_join(joined[1], "x", 1)
        pieces = []
        for base in (0, result.shape[1]):
            pieces.append(both[:, base : base + tok_count])
            pieces.append(both[:, base + tok_count : base + tok_count + mem_count])
        over_z, over_x = after((over_z, over_x), tuple(pieces))
        far = [ring_swap(over_z, "z", 0), ring_swap(over_x, "x", 0)]
        near = [core_swap(over_z), core_swap(over_x)]
        core = lax.axis_index("core")
        codes = []
        for where in (core, 1 - core):
            for group, axis in enumerate(("z", "x")):
                codes.append(4 * where + 2 * group + side_of(lax.axis_index(axis), where, 0))
        codes = jnp.stack(codes).astype(jnp.int32).reshape(1, 4)
        *wide, small = widen([over_z, over_x, *near], codes, width, small_count)
        start = mem_count
        vectors = [small[start + row] for row in range(8)]
        bin_rows = w_in.shape[1] // width
        vectors.append(small[start + 8 : start + 8 + bin_rows].reshape(-1))
        vectors.append(small[:mem_count])
        far, wide, vectors = lax.optimization_barrier((far, wide, vectors))
        far = [*far, core_swap(far[0]), core_swap(far[1])]
        wide = widen(far, codes ^ 1, width, small_count, wide)
        return *wide, *vectors, *pieces

    def nothing(operands):
        text_zero = jnp.zeros(tokens.shape, BF16)
        mem_zero = jnp.zeros(memory.shape, BF16)
        line = jnp.zeros((width,), F32)
        return (
            jnp.zeros(w_qkv.shape, F32),
            jnp.zeros(w_out.shape, F32),
            *[line] * 8,
            jnp.zeros(b_in.shape, F32),
            jnp.zeros(mem_init.shape, F32),
            text_zero,
            mem_zero,
            text_zero,
            mem_zero,
        )

    (
        grad_wqkv,
        grad_wout,
        grad_bquery,
        grad_bvalue,
        grad_gain1,
        grad_bias1,
        grad_bout,
        grad_gain2,
        grad_bias2,
        grad_bdown,
        grad_bin,
        grad_init,
        output,
        mem_output,
        grad_tokens,
        grad_memory,
    ) = lax.cond(
        reset_flags[0] >= 0, attention_back, nothing, (result, g_two, g_inner, sums_two, sums_in)
    )
    grad_down, grad_in = widen_feed(grad_down, grad_in)
    return (
        output,
        mem_output,
        grad_tokens,
        grad_memory,
        grad_init,
        grad_wqkv,
        grad_bquery,
        grad_bvalue,
        grad_wout,
        grad_bout,
        grad_gain1,
        grad_bias1,
        grad_in,
        grad_bin,
        grad_down,
        grad_bdown,
        grad_gain2,
        grad_bias2,
    )


def solution(mesh):
    chips = Mesh(mesh.devices.reshape(4, 4, 4, 2), ALL)
    placed = (
        P(SEG, BLK, None),
        P(SEG, None, None),
        P(),
        P(SEG),
        P(SEG, None),
        *([P()] * 13),
        P(SEG, BLK, None),
        P(SEG, None, None),
    )
    return jax.shard_map(
        local,
        mesh=chips,
        in_specs=placed,
        out_specs=(
            P(SEG, BLK, None),
            P(SEG, None, None),
            P(SEG, BLK, None),
            P(SEG, None, None),
            *([P()] * 14),
        ),
        check_vma=False,
    )
```

profile of v0, /device:TPU:1, one launch (start us, length us, event | category | flops | bytes accessed | tf_op | source)
XLA Modules:
  0.0 263.7 jit_solution(8222457889486261566)
XLA Ops:
  7.3 7.0 %all-to-all-start.1 = ((bf16[8,64,768]{2,1,0:T(8,128)(2,1)}), bf16[8,64,768]{2,1,0:T(8,128)(2,1)S(1)}, u32[]{:S(2)}, u32[]{:S(2)}) async-start(bf16[8,64,768]{2,1,0:T(8,128)(2,1)} %param.22), calls=%async_computation.1 | async-start | bytes 1572864 | tf_op jit(solution)/shard_map/all_to_all | solution.py:684
  15.7 1.2 constant_dynamic-slice_fusion
  20.0 6.6 %all-to-all-done.1 = bf16[8,64,768]{2,1,0:T(8,128)(2,1)S(1)} async-done(((bf16[8,64,768]{2,1,0:T(8,128)(2,1)}), bf16[8,64,768]{2,1,0:T(8,128)(2,1)S(1)}, u32[]{:S(2)}, u32[]{:S(2)}) %all-to-all-start.1) | async-done | bytes 786464 | tf_op jit(solution)/shard_map/all_to_all | solution.py:684
  26.6 4.3 %all-to-all-start.2 = ((bf16[8,64,768]{2,1,0:T(8,128)(2,1)}), bf16[8,64,768]{2,1,0:T(8,128)(2,1)S(1)}, u32[]{:S(2)}, u32[]{:S(2)}) async-start(bf16[8,64,768]{2,1,0:T(8,128)(2,1)} %param.40), calls=%async_computation.2 | async-start | bytes 1572864 | tf_op jit(solution)/shard_map/all_to_all | solution.py:684
  31.2 12.8 %attend.1 = (bf16[544,768]{1,0:T(8,128)(2,1)}, bf16[544,768]{1,0:T(8,128)(2,1)}, bf16[544,768]{1,0:T(8,128)(2,1)}, bf16[544,768]{1,0:T(8,128)(2,1)}, f32[544,128]{1,0:T(8,128)S(1)}, /*index=5*/f32[544,768]{1,0:T(8,128)}) custom-call(bf16[512,768]{1,0:T(8,128)(2,1)S(1)} %bitcast.44, bf16[32,768]{1,0:T(8,128)(2,1)S(1)} %pad.32.mem, bf16[768,2304]{1,0:T(8,128)(2,1)} %w_v.1, ...), custom_call_target="tpu_custom_call" | custom-call | flops 15000000512 | tf_op jit(solution)/shard_map/attend/pallas_call | solution.py:133
  44.0 0.9 copy-done.3
  44.8 25.4 %feed.1 = (bf16[8,96,768]{2,1,0:T(8,128)(2,1)}, f32[544,768]{1,0:T(8,128)}, bf16[544,3072]{1,0:T(8,128)(2,1)}, f32[8,768]{1,0:T(8,128)S(1)}, f32[8,3072]{1,0:T(8...) custom-call(f32[544,768]{1,0:T(8,128)} %get-tuple-element.137.resid, ...), custom_call_target="tpu_custom_call" | custom-call | flops 28000000000 | tf_op jit(solution)/shard_map/feed/pallas_call | solution.py:241
  71.6 175.6 %conditional.1 = (f32[768,2304]{1,0:T(8,128)}, f32[768,768]{1,0:T(8,128)}, f32[768]{0:T(1024)}, f32[768]{0:T(1024)}, f32[768]{0:T(1024)}, /*index=5*/f32[768]{0:...) conditional(s32[]{:T(128)} %bitcast.20, () %tuple.21, ...), branch_computations={%region_0.1_spmd, %region_1.2_spmd} | conditional | flops 41021874176 | bytes 103673672 | solution.py:850
  86.2 33.5 %backward.1 = (bf16[10240,128]{1,0:T(8,128)(2,1)}, bf16[10240,128]{1,0:T(8,128)(2,1)}, bf16[8,192,768]{2,1,0:T(8,128)(2,1)}) custom-call(f32[544,768]{1,0:T(8,128)} %get-tuple-element.41.g_two, bf16[544,3072]{1,0:T(8,128)(2,1)} %get-tuple-element.42.g_inner, bf16[768,3072]{1,0:T(8,128)(2,1)} %get-tuple-element.43.w_in, f32[544,768]{1,0:T(8,128)} %get-tuple-element.44.resid, ...), custom_call_target="tpu_custom_call" | custom-call | flops 32999999488 | tf_op jit(solution)/shard_map/cond/branch_1_fun/backward/pallas_call | solution.py:458
  120.1 4.7 %collective-permute-done = bf16[10240,128]{1,0:T(8,128)(2,1)S(1)} collective-permute-done((bf16[10240,128]{1,0:T(8,128)(2,1)}, bf16[10240,128]{1,0:T(8,128)(2,1)S(1)}, u32[]{:S(2)}, u32[]{:S(2)}) %collective-permute-start) | collective-permute-done | bytes 2621472 | tf_op jit(solution)/shard_map/cond/branch_1_fun/ppermute | solution.py:654
  124.8 1.5 copy-done.2
  126.3 3.2 %add_convert_fusion.1 = (bf16[2560,128]{1,0:T(8,128)(2,1)S(1)}, bf16[2560,128]{1,0:T(8,128)(2,1)S(1)}, bf16[2560,128]{1,0:T(8,128)(2,1)S(1)}, bf16[2560,128]{1,0:T(8,128)(2,1)S(1)}) fusion(bf16[10240,128]{1,0:T(8,128)(2,1)} %copy-done.2, s32[]{:T(128)S(6)} %select_n.222, bf16[10240,128]{1,0:T(8,128)(2,1)} %get-tuple-element.61, s32[]{:T(128)S(6)} %select_n.225, ...), kind=kLoop, calls=%fused_computation.1 | loop fusion | flops 5242880 | bytes 7864336 | tf_op jit(solution)/shard_map/cond/branch_1_fun/convert_element_type | solution.py:658
  129.5 2.9 %collective-permute-start.1 = (bf16[2560,128]{1,0:T(8,128)(2,1)S(1)}, bf16[2560,128]{1,0:T(8,128)(2,1)}, u32[]{:S(2)}, u32[]{:S(2)}) collective-permute-start(bf16[2560,128]{1,0:T(8,128)(2,1)S(1)} %get-tuple-element.255), channel_id=1, source_target_pairs={{0,2},{1,7},{2,0},{3,5},{4,6},{5,3},{6,4},{7,1},{8,10},{9,15},{10,... | collective-permute-start | bytes 1966088 | tf_op jit(solution)/shard_map/cond/branch_1_fun/ppermute | solution.py:650
  132.4 2.6 collective-permute-start.3
  135.0 5.5 %collective-permute-done.1 = bf16[2560,128]{1,0:T(8,128)(2,1)} collective-permute-done((bf16[2560,128]{1,0:T(8,128)(2,1)S(1)}, bf16[2560,128]{1,0:T(8,128)(2,1)}, u32[]{:S(2)}, u32[]{:S(2)}) %collective-permute-start.1) | collective-permute-done | bytes 655392 | tf_op jit(solution)/shard_map/cond/branch_1_fun/ppermute | solution.py:650
  140.5 2.0 add_convert_fusion.7
  143.4 0.9 add_convert_fusion.5
  144.3 0.8 collective-permute-start.4
  145.1 7.9 %all-to-all-start = ((bf16[8,192,768]{2,1,0:T(8,128)(2,1)}), bf16[8,192,768]{2,1,0:T(8,128)(2,1)S(1)}, u32[]{:S(2)}, u32[]{:S(2)}) async-start(bf16[8,192,768]{2,1,0:T(8,128)(2,1)} %get-tuple-element.64), calls=%async_computation | async-start | bytes 4718592 | tf_op jit(solution)/shard_map/cond/branch_1_fun/all_to_all | solution.py:779
  153.0 1.1 fusion.2
  154.2 2.8 %collective-permute-start.5 = (bf16[2,640,128]{2,1,0:T(8,128)(2,1)S(1)}, bf16[2,640,128]{2,1,0:T(8,128)(2,1)S(1)}, u32[]{:S(2)}, u32[]{:S(2)}) collective-permute-start(bf16[2,640,128]{2,1,0:T(8,128)(2,1)S(1)} %pad_maximum_fusion), channel_id=1, source_target_pairs={{0,32},{1,97},{32,0},{33,65},{64,96},{65,33},{96,64},{97,1},{2,34}... | collective-permute-start | bytes 983048 | tf_op jit(solution)/shard_map/cond/branch_1_fun/ppermute | solution.py:650
  157.1 4.8 %collective-permute-done.5 = bf16[2,640,128]{2,1,0:T(8,128)(2,1)S(1)} collective-permute-done((bf16[2,640,128]{2,1,0:T(8,128)(2,1)S(1)}, bf16[2,640,128]{2,1,0:T(8,128)(2,1)S(1)}, u32[]{:S(2)}, u32[]{:S(2)}) %collective-permute-start.5) | collective-permute-done | bytes 327712 | tf_op jit(solution)/shard_map/cond/branch_1_fun/ppermute | solution.py:650
  162.0 4.6 %collective-permute-done.6 = bf16[2,320,128]{2,1,0:T(8,128)(2,1)S(1)} collective-permute-done((bf16[2,320,128]{2,1,0:T(8,128)(2,1)S(1)}, bf16[2,320,128]{2,1,0:T(8,128)(2,1)S(1)}, u32[]{:S(2)}, u32[]{:S(2)}) %collective-permute-start.6) | collective-permute-done | bytes 163872 | tf_op jit(solution)/shard_map/cond/branch_1_fun/ppermute | solution.py:650
  167.1 2.3 collective-permute-start.9
  169.4 2.3 collective-permute-done.7
  171.8 11.9 %collective-permute-done.9 = bf16[320,128]{1,0:T(8,128)(2,1)S(1)} collective-permute-done((bf16[320,128]{1,0:T(8,128)(2,1)S(1)}, bf16[320,128]{1,0:T(8,128)(2,1)S(1)}, u32[]{:S(2)}, u32[]{:S(2)}) %collective-permute-start.9) | collective-permute-done | bytes 81952 | tf_op jit(solution)/shard_map/cond/branch_1_fun/ppermute | solution.py:650
  183.9 3.2 %collective-permute-done.10 = bf16[320,128]{1,0:T(8,128)(2,1)S(1)} collective-permute-done((bf16[320,128]{1,0:T(8,128)(2,1)S(1)}, bf16[320,128]{1,0:T(8,128)(2,1)S(1)}, u32[]{:S(2)}, u32[]{:S(2)}) %collective-permute-start.10) | collective-permute-done | bytes 81952 | tf_op jit(solution)/shard_map/cond/branch_1_fun/ppermute | solution.py:650
  187.2 1.2 collective-permute-start.11
  188.4 4.2 %collective-permute-done.11 = bf16[2,320,128]{2,1,0:T(8,128)(2,1)S(1)} collective-permute-done((bf16[2,320,128]{2,1,0:T(8,128)(2,1)S(1)}, bf16[2,320,128]{2,1,0:T(8,128)(2,1)S(1)}, u32[]{:S(2)}, u32[]{:S(2)}) %collective-permute-start.11) | collective-permute-done | bytes 163872 | tf_op jit(solution)/shard_map/cond/branch_1_fun/ppermute | solution.py:650
  192.7 3.0 %collective-permute-start.12 = (bf16[2,640,128]{2,1,0:T(8,128)(2,1)S(1)}, bf16[2,640,128]{2,1,0:T(8,128)(2,1)S(1)}, u32[]{:S(2)}, u32[]{:S(2)}) collective-permute-start(bf16[2,640,128]{2,1,0:T(8,128)(2,1)S(1)} %maximum_select_fusion.3), channel_id=1, source_target_pairs={{0,32},{1,97},{32,0},{33,65},{64,96},{65,33},{96,64},{97,1},{2,34}... | collective-permute-start | bytes 983048 | tf_op jit(solution)/shard_map/cond/branch_1_fun/ppermute | solution.py:650
  195.7 5.4 %collective-permute-done.12 = bf16[2,640,128]{2,1,0:T(8,128)(2,1)S(1)} collective-permute-done((bf16[2,640,128]{2,1,0:T(8,128)(2,1)S(1)}, bf16[2,640,128]{2,1,0:T(8,128)(2,1)S(1)}, u32[]{:S(2)}, u32[]{:S(2)}) %collective-permute-start.12) | collective-permute-done | bytes 327712 | tf_op jit(solution)/shard_map/cond/branch_1_fun/ppermute | solution.py:650
  202.1 1.2 fusion.16
  203.6 3.7 %collective-permute-done.14 = bf16[1280,128]{1,0:T(8,128)(2,1)S(1)} collective-permute-done((bf16[1280,128]{1,0:T(8,128)(2,1)S(1)}, bf16[1280,128]{1,0:T(8,128)(2,1)S(1)}, u32[]{:S(2)}, u32[]{:S(2)}) %collective-permute-start.14) | collective-permute-done | bytes 327712 | tf_op jit(solution)/shard_map/cond/branch_1_fun/ppermute | solution.py:650
  207.5 2.1 collective-permute-done.13
  209.8 7.8 %collective-permute-start.17 = (bf16[2560,128]{1,0:T(8,128)(2,1)S(1)}, bf16[2560,128]{1,0:T(8,128)(2,1)}, u32[]{:S(2)}, u32[]{:S(2)}) collective-permute-start(bf16[2560,128]{1,0:T(8,128)(2,1)S(1)} %maximum_select_fusion.1.refs_0_), channel_id=1, source_target_pairs={{0,1},{1,0},{2,3},{3,2},{4,5},{5,4},{6,7},{7,6},{8,9},{9,8},{10,11... | collective-permute-start | bytes 1966088 | tf_op jit(solution)/shard_map/cond/branch_1_fun/ppermute | solution.py:654
  217.7 3.4 %collective-permute-start.15 = (bf16[2560,128]{1,0:T(8,128)(2,1)S(1)}, bf16[2560,128]{1,0:T(8,128)(2,1)S(1)}, u32[]{:S(2)}, u32[]{:S(2)}) collective-permute-start(bf16[2560,128]{1,0:T(8,128)(2,1)S(1)} %maximum_select_fusion.1.refs_0_), channel_id=1, source_target_pairs={{0,2},{1,7},{2,0},{3,5},{4,6},{5,3},{6,4},{7,1},{8,10},{9,15},{10,... | collective-permute-start | bytes 1966088 | tf_op jit(solution)/shard_map/cond/branch_1_fun/ppermute | solution.py:650
  221.1 1.3 collective-permute-start.16
  222.9 4.7 %widen.2 = (f32[768,2304]{1,0:T(8,128)}, f32[768,768]{1,0:T(8,128)}, f32[32,768]{1,0:T(8,128)}) custom-call(bf16[2560,128]{1,0:T(8,128)(2,1)} %copy-done.5, bf16[2560,128]{1,0:T(8,128)(2,1)} %copy-done.4, bf16[2560,128]{1,0:T(8,128)(2,1)} %collective-permute-done.17.refs_2_, bf16[2560,128]{1,0:T(8,128)(2,1)} %collective-permute-done.18.refs_3_, ...), custom_call_target="tpu_custom_call" | custom-call | flops 4000000000 | tf_op jit(solution)/shard_map/cond/branch_1_fun/widen/pallas_call | solution.py:561
  227.7 0.7 slice.60
  228.4 1.5 slice.61
  229.9 1.6 slice_reduce_fusion
  231.5 3.7 %collective-permute-done.15.refs_0_ = bf16[2560,128]{1,0:T(8,128)(2,1)S(1)} collective-permute-done((bf16[2560,128]{1,0:T(8,128)(2,1)S(1)}, bf16[2560,128]{1,0:T(8,128)(2,1)S(1)}, u32[]{:S(2)}, u32[]{:S(2)}) %collective-permute-start.15) | collective-permute-done | bytes 655392 | tf_op jit(solution)/shard_map/cond/branch_1_fun/ppermute | solution.py:650
  235.3 3.6 %collective-permute-done.16.refs_1_ = bf16[2560,128]{1,0:T(8,128)(2,1)S(1)} collective-permute-done((bf16[2560,128]{1,0:T(8,128)(2,1)S(1)}, bf16[2560,128]{1,0:T(8,128)(2,1)S(1)}, u32[]{:S(2)}, u32[]{:S(2)}) %collective-permute-start.16) | collective-permute-done | bytes 655392 | tf_op jit(solution)/shard_map/cond/branch_1_fun/ppermute | solution.py:650
  240.0 0.7 copy.63
  241.5 0.9 collective-permute-done.20.refs_3_
  242.4 0.8 copy-done.27
  243.2 4.0 %widen.3 = (f32[768,2304]{1,0:T(8,128)}, f32[768,768]{1,0:T(8,128)}) custom-call(bf16[2560,128]{1,0:T(8,128)(2,1)} %copy-done.24, bf16[2560,128]{1,0:T(8,128)(2,1)} %copy-done.25, bf16[2560,128]{1,0:T(8,128)(2,1)} %copy-done.26, bf16[2560,128]{1,0:T(8,128)(2,1)} %copy-done.27, ...), custom_call_target="tpu_custom_call", output_to_operand_aliasing={{0}: (5, {}), {1}: (6, {})} | custom-call | flops 4000000000 | tf_op jit(solution)/shard_map/cond/branch_1_fun/widen/pallas_call | solution.py:561
  247.3 9.2 %widen_feed.1 = (f32[3072,768]{1,0:T(8,128)}, f32[768,3072]{1,0:T(8,128)}) custom-call(bf16[3072,768]{1,0:T(8,128)(2,1)} %get-tuple-element.251.down, bf16[4,768,768]{2,1,0:T(8,128)(2,1)} %get-tuple-element.252.inward), custom_call_target="tpu_custom_call" | custom-call | flops 8999999488 | tf_op jit(solution)/shard_map/widen_feed/pallas_call | solution.py:608
  (123 shorter events, 11.5 us)
Async XLA Ops:
  7.2 7.7 %copy-start = (s32[8,512]{1,0:T(8,128)S(1)}, s32[8,512]{1,0:T(8,128)}, u32[]{:S(2)}) copy-start(s32[8,512]{1,0:T(8,128)} %param.26) | copy-start | bytes 49156
  7.2 7.1 %copy-start.14 = (s32[8]{0:T(128)S(1)}, s32[8]{0:T(128)}, u32[]{:S(2)}) copy-start(s32[8]{0:T(128)} %param.25) | copy-start | bytes 100
  7.2 9.7 %copy-start.15 = (bf16[768]{0:T(1024)(128)(2,1)S(1)}, bf16[768]{0:T(1024)(128)(2,1)}, u32[]{:S(2)}) copy-start(bf16[768]{0:T(1024)(128)(2,1)} %param.28) | copy-start | bytes 4612
  7.2 9.9 %copy-start.16 = (bf16[768]{0:T(1024)(128)(2,1)S(1)}, bf16[768]{0:T(1024)(128)(2,1)}, u32[]{:S(2)}) copy-start(bf16[768]{0:T(1024)(128)(2,1)} %param.29) | copy-start | bytes 4612
  7.2 10.1 %copy-start.17 = (bf16[768]{0:T(1024)(128)(2,1)S(1)}, bf16[768]{0:T(1024)(128)(2,1)}, u32[]{:S(2)}) copy-start(bf16[768]{0:T(1024)(128)(2,1)} %param.31) | copy-start | bytes 4612
  7.3 10.3 %copy-start.18 = (bf16[768]{0:T(1024)(128)(2,1)S(1)}, bf16[768]{0:T(1024)(128)(2,1)}, u32[]{:S(2)}) copy-start(bf16[768]{0:T(1024)(128)(2,1)} %param.32) | copy-start | bytes 4612
  7.3 10.5 %copy-start.19 = (bf16[768]{0:T(1024)(128)(2,1)S(1)}, bf16[768]{0:T(1024)(128)(2,1)}, u32[]{:S(2)}) copy-start(bf16[768]{0:T(1024)(128)(2,1)} %param.33) | copy-start | bytes 4612
  7.3 10.7 %copy-start.20 = (bf16[768]{0:T(1024)(128)(2,1)S(1)}, bf16[768]{0:T(1024)(128)(2,1)}, u32[]{:S(2)}) copy-start(bf16[768]{0:T(1024)(128)(2,1)} %param.37) | copy-start | bytes 4612
  7.3 10.9 %copy-start.21 = (bf16[768]{0:T(1024)(128)(2,1)S(1)}, bf16[768]{0:T(1024)(128)(2,1)}, u32[]{:S(2)}) copy-start(bf16[768]{0:T(1024)(128)(2,1)} %param.38) | copy-start | bytes 4612
  7.3 11.1 %copy-start.22 = (bf16[768]{0:T(1024)(128)(2,1)S(1)}, bf16[768]{0:T(1024)(128)(2,1)}, u32[]{:S(2)}) copy-start(bf16[768]{0:T(1024)(128)(2,1)} %param.39) | copy-start | bytes 4612
  7.3 11.3 %copy-start.6 = (bf16[20,768]{1,0:T(8,128)(2,1)S(1)}, bf16[20,768]{1,0:T(8,128)(2,1)}, u32[]{:S(2)}) copy-start(bf16[20,768]{1,0:T(8,128)(2,1)} %param.24) | copy-start | bytes 92164
  7.3 11.3 %copy-start.8 = (bf16[3072]{0:T(1024)(128)(2,1)S(1)}, bf16[3072]{0:T(1024)(128)(2,1)}, u32[]{:S(2)}) copy-start(bf16[3072]{0:T(1024)(128)(2,1)} %param.35) | copy-start | bytes 18436
  7.3 19.2 %all-to-all-start.1 = ((bf16[8,64,768]{2,1,0:T(8,128)(2,1)}), bf16[8,64,768]{2,1,0:T(8,128)(2,1)S(1)}, u32[]{:S(2)}, u32[]{:S(2)}) async-start(bf16[8,64,768]{2,1,0:T(8,128)(2,1)} %param.22), calls=%async_computation.1 | async-start | bytes 1572864 | tf_op jit(solution)/shard_map/all_to_all | solution.py:684
  19.4 11.7 %copy-start.23 = (bf16[768,768]{1,0:T(8,128)(2,1)S(1)}, bf16[768,768]{1,0:T(8,128)(2,1)}, u32[]{:S(2)}) copy-start(bf16[768,768]{1,0:T(8,128)(2,1)} %w_out.1) | copy-start | bytes 3538948
  26.6 17.4 %all-to-all-start.2 = ((bf16[8,64,768]{2,1,0:T(8,128)(2,1)}), bf16[8,64,768]{2,1,0:T(8,128)(2,1)S(1)}, u32[]{:S(2)}, u32[]{:S(2)}) async-start(bf16[8,64,768]{2,1,0:T(8,128)(2,1)} %param.40), calls=%async_computation.2 | async-start | bytes 1572864 | tf_op jit(solution)/shard_map/all_to_all | solution.py:684
  30.9 216.4 %all-reduce.11.cloned.1.call-start = ((), (), s32[]{:S(2)}) async-start(), calls=%async_computation.3 | async-start | bytes 18874368 | tf_op jit(solution)/shard_map/psum | solution.py:745
  119.6 5.2 %collective-permute-start = (bf16[10240,128]{1,0:T(8,128)(2,1)}, bf16[10240,128]{1,0:T(8,128)(2,1)S(1)}, u32[]{:S(2)}, u32[]{:S(2)}) collective-permute-start(bf16[10240,128]{1,0:T(8,128)(2,1)} %get-tuple-element.62), channel_id=1, source_target_pairs={{0,1},{1,0},{2,3},{3,2},{4,5},{5,4},{6,7},{7,6},{8,9},{9,8},{10,11... | collective-permute-start | bytes 7864328 | tf_op jit(solution)/shard_map/cond/branch_1_fun/ppermute | solution.py:654
  129.5 11.0 %collective-permute-start.1 = (bf16[2560,128]{1,0:T(8,128)(2,1)S(1)}, bf16[2560,128]{1,0:T(8,128)(2,1)}, u32[]{:S(2)}, u32[]{:S(2)}) collective-permute-start(bf16[2560,128]{1,0:T(8,128)(2,1)S(1)} %get-tuple-element.255), channel_id=1, source_target_pairs={{0,2},{1,7},{2,0},{3,5},{4,6},{5,3},{6,4},{7,1},{8,10},{9,15},{10,... | collective-permute-start | bytes 1966088 | tf_op jit(solution)/shard_map/cond/branch_1_fun/ppermute | solution.py:650
  132.4 10.9 %collective-permute-start.3 = (bf16[2560,128]{1,0:T(8,128)(2,1)S(1)}, bf16[2560,128]{1,0:T(8,128)(2,1)S(1)}, u32[]{:S(2)}, u32[]{:S(2)}) collective-permute-start(bf16[2560,128]{1,0:T(8,128)(2,1)S(1)} %get-tuple-element.254), channel_id=1, source_target_pairs={{0,8},{1,25},{8,0},{9,17},{16,24},{17,9},{24,16},{25,1},{2,10},{3,... | collective-permute-start | bytes 1966088 | tf_op jit(solution)/shard_map/cond/branch_1_fun/ppermute | solution.py:650
  142.5 10.5 %collective-permute-start.2 = (bf16[1280,128]{1,0:T(8,128)(2,1)}, bf16[1280,128]{1,0:T(8,128)(2,1)}, u32[]{:S(2)}, u32[]{:S(2)}) collective-permute-start(bf16[1280,128]{1,0:T(8,128)(2,1)} %get-tuple-element.264), channel_id=1, source_target_pairs={{0,6},{1,3},{2,4},{3,1},{4,2},{5,7},{6,0},{7,5},{8,14},{9,11},{10,... | collective-permute-start | bytes 983048 | tf_op jit(solution)/shard_map/cond/branch_1_fun/ppermute | solution.py:650
  144.3 9.8 %collective-permute-start.4 = (bf16[1280,128]{1,0:T(8,128)(2,1)}, bf16[1280,128]{1,0:T(8,128)(2,1)S(1)}, u32[]{:S(2)}, u32[]{:S(2)}) collective-permute-start(bf16[1280,128]{1,0:T(8,128)(2,1)} %get-tuple-element.262), channel_id=1, source_target_pairs={{0,24},{1,9},{8,16},{9,1},{16,8},{17,25},{24,0},{25,17},{2,26},{3,... | collective-permute-start | bytes 983048 | tf_op jit(solution)/shard_map/cond/branch_1_fun/ppermute | solution.py:650
  145.1 42.0 %all-to-all-start = ((bf16[8,192,768]{2,1,0:T(8,128)(2,1)}), bf16[8,192,768]{2,1,0:T(8,128)(2,1)S(1)}, u32[]{:S(2)}, u32[]{:S(2)}) async-start(bf16[8,192,768]{2,1,0:T(8,128)(2,1)} %get-tuple-element.64), calls=%async_computation | async-start | bytes 4718592 | tf_op jit(solution)/shard_map/cond/branch_1_fun/all_to_all | solution.py:779
  154.2 7.6 %collective-permute-start.5 = (bf16[2,640,128]{2,1,0:T(8,128)(2,1)S(1)}, bf16[2,640,128]{2,1,0:T(8,128)(2,1)S(1)}, u32[]{:S(2)}, u32[]{:S(2)}) collective-permute-start(bf16[2,640,128]{2,1,0:T(8,128)(2,1)S(1)} %pad_maximum_fusion), channel_id=1, source_target_pairs={{0,32},{1,97},{32,0},{33,65},{64,96},{65,33},{96,64},{97,1},{2,34}... | collective-permute-start | bytes 983048 | tf_op jit(solution)/shard_map/cond/branch_1_fun/ppermute | solution.py:650
  161.9 4.7 %collective-permute-start.6 = (bf16[2,320,128]{2,1,0:T(8,128)(2,1)S(1)}, bf16[2,320,128]{2,1,0:T(8,128)(2,1)S(1)}, u32[]{:S(2)}, u32[]{:S(2)}) collective-permute-start(bf16[2,320,128]{2,1,0:T(8,128)(2,1)S(1)} %get-tuple-element.268), channel_id=1, source_target_pairs={{0,96},{1,33},{32,64},{33,1},{64,32},{65,97},{96,0},{97,65},{2,98}... | collective-permute-start | bytes 491528 | tf_op jit(solution)/shard_map/cond/branch_1_fun/ppermute | solution.py:650
  166.7 5.0 %collective-permute-start.7 = (bf16[320,128]{1,0:T(8,128)(2,1)S(1)}, bf16[320,128]{1,0:T(8,128)(2,1)S(1)}, u32[]{:S(2)}, u32[]{:S(2)}) collective-permute-start(bf16[320,128]{1,0:T(8,128)(2,1)S(1)} %get-tuple-element.273), channel_id=1, source_target_pairs={{0,8},{1,25},{8,0},{9,17},{16,24},{17,9},{24,16},{25,1},{2,10},{3,... | collective-permute-start | bytes 245768 | tf_op jit(solution)/shard_map/cond/branch_1_fun/ppermute | solution.py:650
  167.1 16.6 %collective-permute-start.9 = (bf16[320,128]{1,0:T(8,128)(2,1)S(1)}, bf16[320,128]{1,0:T(8,128)(2,1)S(1)}, u32[]{:S(2)}, u32[]{:S(2)}) collective-permute-start(bf16[320,128]{1,0:T(8,128)(2,1)S(1)} %get-tuple-element.274), channel_id=1, source_target_pairs={{0,2},{1,7},{2,0},{3,5},{4,6},{5,3},{6,4},{7,1},{8,10},{9,15},{10,... | collective-permute-start | bytes 245768 | tf_op jit(solution)/shard_map/cond/branch_1_fun/ppermute | solution.py:650
  171.8 12.1 %collective-permute-start.8 = (bf16[320,128]{1,0:T(8,128)(2,1)S(1)}, bf16[320,128]{1,0:T(8,128)(2,1)S(1)}, u32[]{:S(2)}, u32[]{:S(2)}) collective-permute-start(bf16[320,128]{1,0:T(8,128)(2,1)S(1)} %add_convert_fusion.18), channel_id=1, source_target_pairs={{0,24},{1,9},{8,16},{9,1},{16,8},{17,25},{24,0},{25,17},{2,26},{3,... | collective-permute-start | bytes 245768 | tf_op jit(solution)/shard_map/cond/branch_1_fun/ppermute | solution.py:650
  183.7 3.4 %collective-permute-start.10 = (bf16[320,128]{1,0:T(8,128)(2,1)S(1)}, bf16[320,128]{1,0:T(8,128)(2,1)S(1)}, u32[]{:S(2)}, u32[]{:S(2)}) collective-permute-start(bf16[320,128]{1,0:T(8,128)(2,1)S(1)} %add_convert_fusion.15), channel_id=1, source_target_pairs={{0,6},{1,3},{2,4},{3,1},{4,2},{5,7},{6,0},{7,5},{8,14},{9,11},{10,... | collective-permute-start | bytes 245768 | tf_op jit(solution)/shard_map/cond/branch_1_fun/ppermute | solution.py:650
  187.2 5.4 %collective-permute-start.11 = (bf16[2,320,128]{2,1,0:T(8,128)(2,1)S(1)}, bf16[2,320,128]{2,1,0:T(8,128)(2,1)S(1)}, u32[]{:S(2)}, u32[]{:S(2)}) collective-permute-start(bf16[2,320,128]{2,1,0:T(8,128)(2,1)S(1)} %pad_maximum_fusion.1), channel_id=1, source_target_pairs={{0,96},{1,33},{32,64},{33,1},{64,32},{65,97},{96,0},{97,65},{2,98}... | collective-permute-start | bytes 491528 | tf_op jit(solution)/shard_map/cond/branch_1_fun/ppermute | solution.py:650
  192.7 8.4 %collective-permute-start.12 = (bf16[2,640,128]{2,1,0:T(8,128)(2,1)S(1)}, bf16[2,640,128]{2,1,0:T(8,128)(2,1)S(1)}, u32[]{:S(2)}, u32[]{:S(2)}) collective-permute-start(bf16[2,640,128]{2,1,0:T(8,128)(2,1)S(1)} %maximum_select_fusion.3), channel_id=1, source_target_pairs={{0,32},{1,97},{32,0},{33,65},{64,96},{65,33},{96,64},{97,1},{2,34}... | collective-permute-start | bytes 983048 | tf_op jit(solution)/shard_map/cond/branch_1_fun/ppermute | solution.py:650
  201.4 6.0 %collective-permute-start.14 = (bf16[1280,128]{1,0:T(8,128)(2,1)S(1)}, bf16[1280,128]{1,0:T(8,128)(2,1)S(1)}, u32[]{:S(2)}, u32[]{:S(2)}) collective-permute-start(bf16[1280,128]{1,0:T(8,128)(2,1)S(1)} %get-tuple-element.265), channel_id=1, source_target_pairs={{0,24},{1,9},{8,16},{9,1},{16,8},{17,25},{24,0},{25,17},{2,26},{3,... | collective-permute-start | bytes 983048 | tf_op jit(solution)/shard_map/cond/branch_1_fun/ppermute | solution.py:650
  203.4 6.2 %collective-permute-start.13 = (bf16[1280,128]{1,0:T(8,128)(2,1)S(1)}, bf16[1280,128]{1,0:T(8,128)(2,1)S(1)}, u32[]{:S(2)}, u32[]{:S(2)}) collective-permute-start(bf16[1280,128]{1,0:T(8,128)(2,1)S(1)} %get-tuple-element.266), channel_id=1, source_target_pairs={{0,6},{1,3},{2,4},{3,1},{4,2},{5,7},{6,0},{7,5},{8,14},{9,11},{10,... | collective-permute-start | bytes 983048 | tf_op jit(solution)/shard_map/cond/branch_1_fun/ppermute | solution.py:650
  207.5 15.4 %copy-start.4 = (bf16[2560,128]{1,0:T(8,128)(2,1)}, bf16[2560,128]{1,0:T(8,128)(2,1)S(1)}, u32[]{:S(2)}) copy-start(bf16[2560,128]{1,0:T(8,128)(2,1)S(1)} %maximum_select_fusion.2.refs_1_) | copy-start | bytes 1966084 | tf_op jit(solution)/shard_map/cond
  209.8 13.2 %copy-start.5 = (bf16[2560,128]{1,0:T(8,128)(2,1)}, bf16[2560,128]{1,0:T(8,128)(2,1)S(1)}, u32[]{:S(2)}) copy-start(bf16[2560,128]{1,0:T(8,128)(2,1)S(1)} %maximum_select_fusion.1.refs_0_) | copy-start | bytes 1966084 | tf_op jit(solution)/shard_map/cond
  209.8 13.1 %collective-permute-start.17 = (bf16[2560,128]{1,0:T(8,128)(2,1)S(1)}, bf16[2560,128]{1,0:T(8,128)(2,1)}, u32[]{:S(2)}, u32[]{:S(2)}) collective-permute-start(bf16[2560,128]{1,0:T(8,128)(2,1)S(1)} %maximum_select_fusion.1.refs_0_), channel_id=1, source_target_pairs={{0,1},{1,0},{2,3},{3,2},{4,5},{5,4},{6,7},{7,6},{8,9},{9,8},{10,11... | collective-permute-start | bytes 1966088 | tf_op jit(solution)/shard_map/cond/branch_1_fun/ppermute | solution.py:654
  217.6 5.4 %collective-permute-start.18 = (bf16[2560,128]{1,0:T(8,128)(2,1)S(1)}, bf16[2560,128]{1,0:T(8,128)(2,1)}, u32[]{:S(2)}, u32[]{:S(2)}) collective-permute-start(bf16[2560,128]{1,0:T(8,128)(2,1)S(1)} %maximum_select_fusion.2.refs_1_), channel_id=1, source_target_pairs={{0,1},{1,0},{2,3},{3,2},{4,5},{5,4},{6,7},{7,6},{8,9},{9,8},{10,11... | collective-permute-start | bytes 1966088 | tf_op jit(solution)/shard_map/cond/branch_1_fun/ppermute | solution.py:654
  217.7 17.6 %collective-permute-start.15 = (bf16[2560,128]{1,0:T(8,128)(2,1)S(1)}, bf16[2560,128]{1,0:T(8,128)(2,1)S(1)}, u32[]{:S(2)}, u32[]{:S(2)}) collective-permute-start(bf16[2560,128]{1,0:T(8,128)(2,1)S(1)} %maximum_select_fusion.1.refs_0_), channel_id=1, source_target_pairs={{0,2},{1,7},{2,0},{3,5},{4,6},{5,3},{6,4},{7,1},{8,10},{9,15},{10,... | collective-permute-start | bytes 1966088 | tf_op jit(solution)/shard_map/cond/branch_1_fun/ppermute | solution.py:650
  221.1 17.9 %collective-permute-start.16 = (bf16[2560,128]{1,0:T(8,128)(2,1)S(1)}, bf16[2560,128]{1,0:T(8,128)(2,1)S(1)}, u32[]{:S(2)}, u32[]{:S(2)}) collective-permute-start(bf16[2560,128]{1,0:T(8,128)(2,1)S(1)} %maximum_select_fusion.2.refs_1_), channel_id=1, source_target_pairs={{0,8},{1,25},{8,0},{9,17},{16,24},{17,9},{24,16},{25,1},{2,10},{3,... | collective-permute-start | bytes 1966088 | tf_op jit(solution)/shard_map/cond/branch_1_fun/ppermute | solution.py:650
  235.3 7.1 %copy-start.24 = (bf16[2560,128]{1,0:T(8,128)(2,1)}, bf16[2560,128]{1,0:T(8,128)(2,1)S(1)}, u32[]{:S(2)}) copy-start(bf16[2560,128]{1,0:T(8,128)(2,1)S(1)} %collective-permute-done.15.refs_0_) | copy-start | bytes 1966084 | tf_op jit(solution)/shard_map/cond
  238.9 2.6 collective-permute-start.19
  238.9 3.5 %collective-permute-start.20 = (bf16[2560,128]{1,0:T(8,128)(2,1)S(1)}, bf16[2560,128]{1,0:T(8,128)(2,1)S(1)}, u32[]{:S(2)}, u32[]{:S(2)}) collective-permute-start(bf16[2560,128]{1,0:T(8,128)(2,1)S(1)} %collective-permute-done.16.refs_1_), channel_id=1, source_target_pairs={{0,1},{1,0},{2,3},{3,2},{4,5},{5,4},{6,7},{7,6},{8,9},{9,8},{10,11... | collective-permute-start | bytes 1966088 | tf_op jit(solution)/shard_map/cond/branch_1_fun/ppermute | solution.py:654
  247.2 9.4 %copy-start.7 = (f32[3072]{0:T(1024)}, f32[3072]{0:T(1024)S(1)}, u32[]{:S(2)}) copy-start(f32[3072]{0:T(1024)S(1)} %get-tuple-element.236) | copy-start | bytes 36868
  247.2 9.4 %copy-start.9 = (f32[768]{0:T(1024)}, f32[768]{0:T(1024)S(1)}, u32[]{:S(2)}) copy-start(f32[768]{0:T(1024)S(1)} %get-tuple-element.238) | copy-start | bytes 9220
  247.2 9.4 %copy-start.10 = (f32[768]{0:T(1024)}, f32[768]{0:T(1024)S(1)}, u32[]{:S(2)}) copy-start(f32[768]{0:T(1024)S(1)} %get-tuple-element.240) | copy-start | bytes 9220
  247.3 9.4 %copy-start.11 = (f32[768]{0:T(1024)}, f32[768]{0:T(1024)S(1)}, u32[]{:S(2)}) copy-start(f32[768]{0:T(1024)S(1)} %get-tuple-element.239) | copy-start | bytes 9220
  247.3 9.3 %copy-start.12 = (f32[768]{0:T(1024)}, f32[768]{0:T(1024)S(1)}, u32[]{:S(2)}) copy-start(f32[768]{0:T(1024)S(1)} %get-tuple-element.232) | copy-start | bytes 9220
  247.3 9.3 %copy-start.13 = (f32[768]{0:T(1024)}, f32[768]{0:T(1024)S(1)}, u32[]{:S(2)}) copy-start(f32[768]{0:T(1024)S(1)} %get-tuple-element.234) | copy-start | bytes 9220
  247.3 9.3 %copy-start.1 = (s32[8,512]{1,0:T(8,128)S(1)}, s32[8,512]{1,0:T(8,128)}, u32[]{:S(2)}) copy-start(s32[8,512]{1,0:T(8,128)} %param.26) | copy-start | bytes 49156
  (5 other events, 7.6 us)
Sparse Core Ops, SparseCore 0:
  70.4 173.8 all-reduce.10
where the time goes:
time: 264 us
  Pallas kernels  89.5 us (34%)
  waiting for transfers between devices  67.7 us (26%)
  starting transfers between devices  50.8 us (19%)
  between operations  15.9 us (6%)
  loops' own time  14.8 us (6%)
  local copies, waits for them, and re-layouts  14.6 us (6%)
  other arithmetic  10.4 us (4%)
    ppermute x16, waiting for transfers between devices, ring_swap(): return lax.ppermute(value, (axis, 'core'), ring_pairs(step))  55.5 us
    pallas_call x1, Pallas kernels, backward(): pl.pallas_call(backward_kernel, grid=(parts + 3,), in_specs=[full, early(...  33.5 us
    pallas_call x1, Pallas kernels, feed(): pl.pallas_call(feed_kernel, grid=(2 * half,), in_specs=[full, whole(lines...  25.4 us
    ppermute x16, starting transfers between devices, ring_swap(): return lax.ppermute(value, (axis, 'core'), ring_pairs(step))  22.6 us
    another operation x1, loops' own time, local(): lax.cond(reset_flags[0] >= 0, attention_back, nothing, (result, g_two, g_...  14.8 us
    pallas_call x1, Pallas kernels, attend(): pl.pallas_call(attend_kernel, grid=(3,), in_specs=[whole(text.shape), who...  12.8 us
    all_to_all x2, starting transfers between devices, to_segments(): return lax.all_to_all(value, BLK, 0, 1, tiled=True)[0]  11.3 us
    pallas_call x1, Pallas kernels, widen_feed(): pl.pallas_call(widen_feed_kernel, in_specs=[hbm, hbm], out_specs=[hbm, hb...  9.23 us
  transfers between devices with their start and end apart: 25, of which 16 were waited for; matrix products, arithmetic and copies ran while one was open for 8% of the time, Pallas kernels for 21%

commit v1 on v0

--- a/solution.py
+++ b/solution.py
@@ -513,9 +513,9 @@
     def copies(place):
         code = codes[0, place]
         in_qkv = code < 6
-        spot = jnp.where(in_qkv, code, code - 6)
-        columns = pl.ds(pl.multiple_of(spot * part, part), part)
+        columns = pl.ds(pl.multiple_of(jnp.minimum(code, 5) * part, part), part)
         to_qkv = pltpu.make_async_copy(wide.at[place], qkv_out.at[:, columns], sems.at[place])
+        columns = pl.ds(pl.multiple_of(jnp.maximum(code - 6, 0) * part, part), part)
         to_out = pltpu.make_async_copy(wide.at[place], out_out.at[:, columns], sems.at[place])
         return in_qkv, to_qkv, to_out
 

time: 264 us -> 264 us (level)
  no operation moved by 1% of the time
where the time goes in v1:
time: 264 us; the launch traced here: 263 us
  Pallas kernels  89.5 us (34%)
  waiting for transfers between devices  67.8 us (26%)
  starting transfers between devices  50.3 us (19%)
  between operations  15.9 us (6%)
  local copies, waits for them, and re-layouts  14.7 us (6%)
  loops' own time  14.7 us (6%)
  other arithmetic  10.4 us (4%)
    ppermute x16, waiting for transfers between devices, ring_swap(): return lax.ppermute(value, (axis, 'core'), ring_pairs(step))  55.7 us
    pallas_call x1, Pallas kernels, backward(): pl.pallas_call(backward_kernel, grid=(parts + 3,), in_specs=[full, early(...  33.5 us
    pallas_call x1, Pallas kernels, feed(): pl.pallas_call(feed_kernel, grid=(2 * half,), in_specs=[full, whole(lines...  25.4 us
    ppermute x16, starting transfers between devices, ring_swap(): return lax.ppermute(value, (axis, 'core'), ring_pairs(step))  22.3 us
    another operation x1, loops' own time, local(): lax.cond(reset_flags[0] >= 0, attention_back, nothing, (result, g_two, g_...  14.7 us
    pallas_call x1, Pallas kernels, attend(): pl.pallas_call(attend_kernel, grid=(3,), in_specs=[whole(text.shape), who...  12.8 us
    all_to_all x2, starting transfers between devices, to_segments(): return lax.all_to_all(value, BLK, 0, 1, tiled=True)[0]  11.3 us
    pallas_call x1, Pallas kernels, widen_feed(): pl.pallas_call(widen_feed_kernel, in_specs=[hbm, hbm], out_specs=[hbm, hb...  9.23 us
  transfers between devices with their start and end apart: 25, of which 16 were waited for; matrix products, arithmetic and copies ran while one was open for 8% of the time, Pallas kernels for 21%

profile of v1, /device:TPU:1, one launch (start us, length us, event | category | flops | bytes accessed | tf_op | source)
XLA Modules:
  0.0 263.4 jit_solution(12151422726795352004)
XLA Ops:
  7.3 7.0 %all-to-all-start.1 = ((bf16[8,64,768]{2,1,0:T(8,128)(2,1)}), bf16[8,64,768]{2,1,0:T(8,128)(2,1)S(1)}, u32[]{:S(2)}, u32[]{:S(2)}) async-start(bf16[8,64,768]{2,1,0:T(8,128)(2,1)} %param.22), calls=%async_computation.1 | async-start | bytes 1572864 | tf_op jit(solution)/shard_map/all_to_all | solution.py:684
  15.7 1.2 constant_dynamic-slice_fusion
  20.0 6.6 %all-to-all-done.1 = bf16[8,64,768]{2,1,0:T(8,128)(2,1)S(1)} async-done(((bf16[8,64,768]{2,1,0:T(8,128)(2,1)}), bf16[8,64,768]{2,1,0:T(8,128)(2,1)S(1)}, u32[]{:S(2)}, u32[]{:S(2)}) %all-to-all-start.1) | async-done | bytes 786464 | tf_op jit(solution)/shard_map/all_to_all | solution.py:684
  26.6 4.3 %all-to-all-start.2 = ((bf16[8,64,768]{2,1,0:T(8,128)(2,1)}), bf16[8,64,768]{2,1,0:T(8,128)(2,1)S(1)}, u32[]{:S(2)}, u32[]{:S(2)}) async-start(bf16[8,64,768]{2,1,0:T(8,128)(2,1)} %param.40), calls=%async_computation.2 | async-start | bytes 1572864 | tf_op jit(solution)/shard_map/all_to_all | solution.py:684
  31.2 12.8 %attend.1 = (bf16[544,768]{1,0:T(8,128)(2,1)}, bf16[544,768]{1,0:T(8,128)(2,1)}, bf16[544,768]{1,0:T(8,128)(2,1)}, bf16[544,768]{1,0:T(8,128)(2,1)}, f32[544,128]{1,0:T(8,128)S(1)}, /*index=5*/f32[544,768]{1,0:T(8,128)}) custom-call(bf16[512,768]{1,0:T(8,128)(2,1)S(1)} %bitcast.44, bf16[32,768]{1,0:T(8,128)(2,1)S(1)} %pad.32.mem, bf16[768,2304]{1,0:T(8,128)(2,1)} %w_v.1, ...), custom_call_target="tpu_custom_call" | custom-call | flops 15000000512 | tf_op jit(solution)/shard_map/attend/pallas_call | solution.py:133
  44.0 0.9 copy-done.3
  44.8 25.4 %feed.1 = (bf16[8,96,768]{2,1,0:T(8,128)(2,1)}, f32[544,768]{1,0:T(8,128)}, bf16[544,3072]{1,0:T(8,128)(2,1)}, f32[8,768]{1,0:T(8,128)S(1)}, f32[8,3072]{1,0:T(8...) custom-call(f32[544,768]{1,0:T(8,128)} %get-tuple-element.137.resid, ...), custom_call_target="tpu_custom_call" | custom-call | flops 28000000000 | tf_op jit(solution)/shard_map/feed/pallas_call | solution.py:241
  71.6 175.3 %conditional.1 = (f32[768,2304]{1,0:T(8,128)}, f32[768,768]{1,0:T(8,128)}, f32[768]{0:T(1024)}, f32[768]{0:T(1024)}, f32[768]{0:T(1024)}, /*index=5*/f32[768]{0:...) conditional(s32[]{:T(128)} %bitcast.20, () %tuple.21, ...), branch_computations={%region_0.1_spmd, %region_1.2_spmd} | conditional | flops 41021874176 | bytes 103673672 | solution.py:850
  86.2 33.5 %backward.1 = (bf16[10240,128]{1,0:T(8,128)(2,1)}, bf16[10240,128]{1,0:T(8,128)(2,1)}, bf16[8,192,768]{2,1,0:T(8,128)(2,1)}) custom-call(f32[544,768]{1,0:T(8,128)} %get-tuple-element.41.g_two, bf16[544,3072]{1,0:T(8,128)(2,1)} %get-tuple-element.42.g_inner, bf16[768,3072]{1,0:T(8,128)(2,1)} %get-tuple-element.43.w_in, f32[544,768]{1,0:T(8,128)} %get-tuple-element.44.resid, ...), custom_call_target="tpu_custom_call" | custom-call | flops 32999999488 | tf_op jit(solution)/shard_map/cond/branch_1_fun/backward/pallas_call | solution.py:458
  120.1 4.8 %collective-permute-done = bf16[10240,128]{1,0:T(8,128)(2,1)S(1)} collective-permute-done((bf16[10240,128]{1,0:T(8,128)(2,1)}, bf16[10240,128]{1,0:T(8,128)(2,1)S(1)}, u32[]{:S(2)}, u32[]{:S(2)}) %collective-permute-start) | collective-permute-done | bytes 2621472 | tf_op jit(solution)/shard_map/cond/branch_1_fun/ppermute | solution.py:654
  124.9 1.5 copy-done.2
  126.3 3.2 %add_convert_fusion.1 = (bf16[2560,128]{1,0:T(8,128)(2,1)S(1)}, bf16[2560,128]{1,0:T(8,128)(2,1)S(1)}, bf16[2560,128]{1,0:T(8,128)(2,1)S(1)}, bf16[2560,128]{1,0:T(8,128)(2,1)S(1)}) fusion(bf16[10240,128]{1,0:T(8,128)(2,1)} %copy-done.2, s32[]{:T(128)S(6)} %select_n.222, bf16[10240,128]{1,0:T(8,128)(2,1)} %get-tuple-element.61, s32[]{:T(128)S(6)} %select_n.225, ...), kind=kLoop, calls=%fused_computation.1 | loop fusion | flops 5242880 | bytes 7864336 | tf_op jit(solution)/shard_map/cond/branch_1_fun/convert_element_type | solution.py:658
  129.5 2.9 %collective-permute-start.1 = (bf16[2560,128]{1,0:T(8,128)(2,1)S(1)}, bf16[2560,128]{1,0:T(8,128)(2,1)}, u32[]{:S(2)}, u32[]{:S(2)}) collective-permute-start(bf16[2560,128]{1,0:T(8,128)(2,1)S(1)} %get-tuple-element.255), channel_id=1, source_target_pairs={{0,2},{1,7},{2,0},{3,5},{4,6},{5,3},{6,4},{7,1},{8,10},{9,15},{10,... | collective-permute-start | bytes 1966088 | tf_op jit(solution)/shard_map/cond/branch_1_fun/ppermute | solution.py:650
  132.4 2.6 collective-permute-start.3
  135.0 5.5 %collective-permute-done.1 = bf16[2560,128]{1,0:T(8,128)(2,1)} collective-permute-done((bf16[2560,128]{1,0:T(8,128)(2,1)S(1)}, bf16[2560,128]{1,0:T(8,128)(2,1)}, u32[]{:S(2)}, u32[]{:S(2)}) %collective-permute-start.1) | collective-permute-done | bytes 655392 | tf_op jit(solution)/shard_map/cond/branch_1_fun/ppermute | solution.py:650
  140.5 2.0 add_convert_fusion.7
  143.4 0.9 add_convert_fusion.5
  144.3 0.8 collective-permute-start.4
  145.1 7.8 %all-to-all-start = ((bf16[8,192,768]{2,1,0:T(8,128)(2,1)}), bf16[8,192,768]{2,1,0:T(8,128)(2,1)S(1)}, u32[]{:S(2)}, u32[]{:S(2)}) async-start(bf16[8,192,768]{2,1,0:T(8,128)(2,1)} %get-tuple-element.64), calls=%async_computation | async-start | bytes 4718592 | tf_op jit(solution)/shard_map/cond/branch_1_fun/all_to_all | solution.py:779
  153.0 1.1 fusion.2
  154.2 2.9 %collective-permute-start.5 = (bf16[2,640,128]{2,1,0:T(8,128)(2,1)S(1)}, bf16[2,640,128]{2,1,0:T(8,128)(2,1)S(1)}, u32[]{:S(2)}, u32[]{:S(2)}) collective-permute-start(bf16[2,640,128]{2,1,0:T(8,128)(2,1)S(1)} %pad_maximum_fusion), channel_id=1, source_target_pairs={{0,32},{1,97},{32,0},{33,65},{64,96},{65,33},{96,64},{97,1},{2,34}... | collective-permute-start | bytes 983048 | tf_op jit(solution)/shard_map/cond/branch_1_fun/ppermute | solution.py:650
  157.1 4.8 %collective-permute-done.5 = bf16[2,640,128]{2,1,0:T(8,128)(2,1)S(1)} collective-permute-done((bf16[2,640,128]{2,1,0:T(8,128)(2,1)S(1)}, bf16[2,640,128]{2,1,0:T(8,128)(2,1)S(1)}, u32[]{:S(2)}, u32[]{:S(2)}) %collective-permute-start.5) | collective-permute-done | bytes 327712 | tf_op jit(solution)/shard_map/cond/branch_1_fun/ppermute | solution.py:650
  162.0 4.6 %collective-permute-done.6 = bf16[2,320,128]{2,1,0:T(8,128)(2,1)S(1)} collective-permute-done((bf16[2,320,128]{2,1,0:T(8,128)(2,1)S(1)}, bf16[2,320,128]{2,1,0:T(8,128)(2,1)S(1)}, u32[]{:S(2)}, u32[]{:S(2)}) %collective-permute-start.6) | collective-permute-done | bytes 163872 | tf_op jit(solution)/shard_map/cond/branch_1_fun/ppermute | solution.py:650
  167.1 2.3 collective-permute-start.9
  169.4 2.3 collective-permute-done.7
  171.8 11.9 %collective-permute-done.9 = bf16[320,128]{1,0:T(8,128)(2,1)S(1)} collective-permute-done((bf16[320,128]{1,0:T(8,128)(2,1)S(1)}, bf16[320,128]{1,0:T(8,128)(2,1)S(1)}, u32[]{:S(2)}, u32[]{:S(2)}) %collective-permute-start.9) | collective-permute-done | bytes 81952 | tf_op jit(solution)/shard_map/cond/branch_1_fun/ppermute | solution.py:650
  183.9 3.2 %collective-permute-done.10 = bf16[320,128]{1,0:T(8,128)(2,1)S(1)} collective-permute-done((bf16[320,128]{1,0:T(8,128)(2,1)S(1)}, bf16[320,128]{1,0:T(8,128)(2,1)S(1)}, u32[]{:S(2)}, u32[]{:S(2)}) %collective-permute-start.10) | collective-permute-done | bytes 81952 | tf_op jit(solution)/shard_map/cond/branch_1_fun/ppermute | solution.py:650
  187.2 1.3 collective-permute-start.11
  188.4 4.3 %collective-permute-done.11 = bf16[2,320,128]{2,1,0:T(8,128)(2,1)S(1)} collective-permute-done((bf16[2,320,128]{2,1,0:T(8,128)(2,1)S(1)}, bf16[2,320,128]{2,1,0:T(8,128)(2,1)S(1)}, u32[]{:S(2)}, u32[]{:S(2)}) %collective-permute-start.11) | collective-permute-done | bytes 163872 | tf_op jit(solution)/shard_map/cond/branch_1_fun/ppermute | solution.py:650
  192.8 2.6 collective-permute-start.12
  195.5 6.0 %collective-permute-done.12 = bf16[2,640,128]{2,1,0:T(8,128)(2,1)S(1)} collective-permute-done((bf16[2,640,128]{2,1,0:T(8,128)(2,1)S(1)}, bf16[2,640,128]{2,1,0:T(8,128)(2,1)S(1)}, u32[]{:S(2)}, u32[]{:S(2)}) %collective-permute-start.12) | collective-permute-done | bytes 327712 | tf_op jit(solution)/shard_map/cond/branch_1_fun/ppermute | solution.py:650
  201.7 0.8 collective-permute-start.14
  202.5 1.2 fusion.16
  203.8 3.9 %collective-permute-done.14 = bf16[1280,128]{1,0:T(8,128)(2,1)S(1)} collective-permute-done((bf16[1280,128]{1,0:T(8,128)(2,1)S(1)}, bf16[1280,128]{1,0:T(8,128)(2,1)S(1)}, u32[]{:S(2)}, u32[]{:S(2)}) %collective-permute-start.14) | collective-permute-done | bytes 327712 | tf_op jit(solution)/shard_map/cond/branch_1_fun/ppermute | solution.py:650
  207.9 2.1 collective-permute-done.13
  210.2 7.6 %collective-permute-start.17 = (bf16[2560,128]{1,0:T(8,128)(2,1)S(1)}, bf16[2560,128]{1,0:T(8,128)(2,1)}, u32[]{:S(2)}, u32[]{:S(2)}) collective-permute-start(bf16[2560,128]{1,0:T(8,128)(2,1)S(1)} %maximum_select_fusion.1.refs_0_), channel_id=1, source_target_pairs={{0,1},{1,0},{2,3},{3,2},{4,5},{5,4},{6,7},{7,6},{8,9},{9,8},{10,11... | collective-permute-start | bytes 1966088 | tf_op jit(solution)/shard_map/cond/branch_1_fun/ppermute | solution.py:654
  217.8 3.4 %collective-permute-start.15 = (bf16[2560,128]{1,0:T(8,128)(2,1)S(1)}, bf16[2560,128]{1,0:T(8,128)(2,1)S(1)}, u32[]{:S(2)}, u32[]{:S(2)}) collective-permute-start(bf16[2560,128]{1,0:T(8,128)(2,1)S(1)} %maximum_select_fusion.1.refs_0_), channel_id=1, source_target_pairs={{0,2},{1,7},{2,0},{3,5},{4,6},{5,3},{6,4},{7,1},{8,10},{9,15},{10,... | collective-permute-start | bytes 1966088 | tf_op jit(solution)/shard_map/cond/branch_1_fun/ppermute | solution.py:650
  221.2 1.4 collective-permute-start.16
  223.3 4.7 %widen.2 = (f32[768,2304]{1,0:T(8,128)}, f32[768,768]{1,0:T(8,128)}, f32[32,768]{1,0:T(8,128)}) custom-call(bf16[2560,128]{1,0:T(8,128)(2,1)} %copy-done.5, bf16[2560,128]{1,0:T(8,128)(2,1)} %copy-done.4, bf16[2560,128]{1,0:T(8,128)(2,1)} %collective-permute-done.17.refs_2_, bf16[2560,128]{1,0:T(8,128)(2,1)} %collective-permute-done.18.refs_3_, ...), custom_call_target="tpu_custom_call" | custom-call | flops 4000000000 | tf_op jit(solution)/shard_map/cond/branch_1_fun/widen/pallas_call | solution.py:561
  228.0 0.7 slice.60
  228.8 1.5 slice.61
  230.3 1.6 slice_reduce_fusion
  231.9 4.5 %collective-permute-done.15.refs_0_ = bf16[2560,128]{1,0:T(8,128)(2,1)S(1)} collective-permute-done((bf16[2560,128]{1,0:T(8,128)(2,1)S(1)}, bf16[2560,128]{1,0:T(8,128)(2,1)S(1)}, u32[]{:S(2)}, u32[]{:S(2)}) %collective-permute-start.15) | collective-permute-done | bytes 655392 | tf_op jit(solution)/shard_map/cond/branch_1_fun/ppermute | solution.py:650
  236.4 2.3 collective-permute-done.16.refs_1_
  239.8 0.7 copy.63
  242.1 0.8 copy-done.27
  243.0 4.0 %widen.3 = (f32[768,2304]{1,0:T(8,128)}, f32[768,768]{1,0:T(8,128)}) custom-call(bf16[2560,128]{1,0:T(8,128)(2,1)} %copy-done.24, bf16[2560,128]{1,0:T(8,128)(2,1)} %copy-done.25, bf16[2560,128]{1,0:T(8,128)(2,1)} %copy-done.26, bf16[2560,128]{1,0:T(8,128)(2,1)} %copy-done.27, ...), custom_call_target="tpu_custom_call", output_to_operand_aliasing={{0}: (5, {}), {1}: (6, {})} | custom-call | flops 4000000000 | tf_op jit(solution)/shard_map/cond/branch_1_fun/widen/pallas_call | solution.py:561
  247.1 9.2 %widen_feed.1 = (f32[3072,768]{1,0:T(8,128)}, f32[768,3072]{1,0:T(8,128)}) custom-call(bf16[3072,768]{1,0:T(8,128)(2,1)} %get-tuple-element.251.down, bf16[4,768,768]{2,1,0:T(8,128)(2,1)} %get-tuple-element.252.inward), custom_call_target="tpu_custom_call" | custom-call | flops 8999999488 | tf_op jit(solution)/shard_map/widen_feed/pallas_call | solution.py:608
  (123 shorter events, 11.4 us)
Async XLA Ops:
  7.2 7.7 %copy-start = (s32[8,512]{1,0:T(8,128)S(1)}, s32[8,512]{1,0:T(8,128)}, u32[]{:S(2)}) copy-start(s32[8,512]{1,0:T(8,128)} %param.26) | copy-start | bytes 49156
  7.2 7.1 %copy-start.14 = (s32[8]{0:T(128)S(1)}, s32[8]{0:T(128)}, u32[]{:S(2)}) copy-start(s32[8]{0:T(128)} %param.25) | copy-start | bytes 100
  7.2 9.7 %copy-start.15 = (bf16[768]{0:T(1024)(128)(2,1)S(1)}, bf16[768]{0:T(1024)(128)(2,1)}, u32[]{:S(2)}) copy-start(bf16[768]{0:T(1024)(128)(2,1)} %param.28) | copy-start | bytes 4612
  7.2 9.9 %copy-start.16 = (bf16[768]{0:T(1024)(128)(2,1)S(1)}, bf16[768]{0:T(1024)(128)(2,1)}, u32[]{:S(2)}) copy-start(bf16[768]{0:T(1024)(128)(2,1)} %param.29) | copy-start | bytes 4612
  7.2 10.1 %copy-start.17 = (bf16[768]{0:T(1024)(128)(2,1)S(1)}, bf16[768]{0:T(1024)(128)(2,1)}, u32[]{:S(2)}) copy-start(bf16[768]{0:T(1024)(128)(2,1)} %param.31) | copy-start | bytes 4612
  7.3 10.3 %copy-start.18 = (bf16[768]{0:T(1024)(128)(2,1)S(1)}, bf16[768]{0:T(1024)(128)(2,1)}, u32[]{:S(2)}) copy-start(bf16[768]{0:T(1024)(128)(2,1)} %param.32) | copy-start | bytes 4612
  7.3 10.5 %copy-start.19 = (bf16[768]{0:T(1024)(128)(2,1)S(1)}, bf16[768]{0:T(1024)(128)(2,1)}, u32[]{:S(2)}) copy-start(bf16[768]{0:T(1024)(128)(2,1)} %param.33) | copy-start | bytes 4612
  7.3 10.7 %copy-start.20 = (bf16[768]{0:T(1024)(128)(2,1)S(1)}, bf16[768]{0:T(1024)(128)(2,1)}, u32[]{:S(2)}) copy-start(bf16[768]{0:T(1024)(128)(2,1)} %param.37) | copy-start | bytes 4612
  7.3 10.9 %copy-start.21 = (bf16[768]{0:T(1024)(128)(2,1)S(1)}, bf16[768]{0:T(1024)(128)(2,1)}, u32[]{:S(2)}) copy-start(bf16[768]{0:T(1024)(128)(2,1)} %param.38) | copy-start | bytes 4612
  7.3 11.1 %copy-start.22 = (bf16[768]{0:T(1024)(128)(2,1)S(1)}, bf16[768]{0:T(1024)(128)(2,1)}, u32[]{:S(2)}) copy-start(bf16[768]{0:T(1024)(128)(2,1)} %param.39) | copy-start | bytes 4612
  7.3 11.3 %copy-start.6 = (bf16[20,768]{1,0:T(8,128)(2,1)S(1)}, bf16[20,768]{1,0:T(8,128)(2,1)}, u32[]{:S(2)}) copy-start(bf16[20,768]{1,0:T(8,128)(2,1)} %param.24) | copy-start | bytes 92164
  7.3 11.3 %copy-start.8 = (bf16[3072]{0:T(1024)(128)(2,1)S(1)}, bf16[3072]{0:T(1024)(128)(2,1)}, u32[]{:S(2)}) copy-start(bf16[3072]{0:T(1024)(128)(2,1)} %param.35) | copy-start | bytes 18436
  7.3 19.2 %all-to-all-start.1 = ((bf16[8,64,768]{2,1,0:T(8,128)(2,1)}), bf16[8,64,768]{2,1,0:T(8,128)(2,1)S(1)}, u32[]{:S(2)}, u32[]{:S(2)}) async-start(bf16[8,64,768]{2,1,0:T(8,128)(2,1)} %param.22), calls=%async_computation.1 | async-start | bytes 1572864 | tf_op jit(solution)/shard_map/all_to_all | solution.py:684
  19.4 11.7 %copy-start.23 = (bf16[768,768]{1,0:T(8,128)(2,1)S(1)}, bf16[768,768]{1,0:T(8,128)(2,1)}, u32[]{:S(2)}) copy-start(bf16[768,768]{1,0:T(8,128)(2,1)} %w_out.1) | copy-start | bytes 3538948
  26.6 17.4 %all-to-all-start.2 = ((bf16[8,64,768]{2,1,0:T(8,128)(2,1)}), bf16[8,64,768]{2,1,0:T(8,128)(2,1)S(1)}, u32[]{:S(2)}, u32[]{:S(2)}) async-start(bf16[8,64,768]{2,1,0:T(8,128)(2,1)} %param.40), calls=%async_computation.2 | async-start | bytes 1572864 | tf_op jit(solution)/shard_map/all_to_all | solution.py:684
  30.9 216.1 %all-reduce.11.cloned.1.call-start = ((), (), s32[]{:S(2)}) async-start(), calls=%async_computation.3 | async-start | bytes 18874368 | tf_op jit(solution)/shard_map/psum | solution.py:745
  119.7 5.2 %collective-permute-start = (bf16[10240,128]{1,0:T(8,128)(2,1)}, bf16[10240,128]{1,0:T(8,128)(2,1)S(1)}, u32[]{:S(2)}, u32[]{:S(2)}) collective-permute-start(bf16[10240,128]{1,0:T(8,128)(2,1)} %get-tuple-element.62), channel_id=1, source_target_pairs={{0,1},{1,0},{2,3},{3,2},{4,5},{5,4},{6,7},{7,6},{8,9},{9,8},{10,11... | collective-permute-start | bytes 7864328 | tf_op jit(solution)/shard_map/cond/branch_1_fun/ppermute | solution.py:654
  129.5 11.0 %collective-permute-start.1 = (bf16[2560,128]{1,0:T(8,128)(2,1)S(1)}, bf16[2560,128]{1,0:T(8,128)(2,1)}, u32[]{:S(2)}, u32[]{:S(2)}) collective-permute-start(bf16[2560,128]{1,0:T(8,128)(2,1)S(1)} %get-tuple-element.255), channel_id=1, source_target_pairs={{0,2},{1,7},{2,0},{3,5},{4,6},{5,3},{6,4},{7,1},{8,10},{9,15},{10,... | collective-permute-start | bytes 1966088 | tf_op jit(solution)/shard_map/cond/branch_1_fun/ppermute | solution.py:650
  132.4 11.0 %collective-permute-start.3 = (bf16[2560,128]{1,0:T(8,128)(2,1)S(1)}, bf16[2560,128]{1,0:T(8,128)(2,1)S(1)}, u32[]{:S(2)}, u32[]{:S(2)}) collective-permute-start(bf16[2560,128]{1,0:T(8,128)(2,1)S(1)} %get-tuple-element.254), channel_id=1, source_target_pairs={{0,8},{1,25},{8,0},{9,17},{16,24},{17,9},{24,16},{25,1},{2,10},{3,... | collective-permute-start | bytes 1966088 | tf_op jit(solution)/shard_map/cond/branch_1_fun/ppermute | solution.py:650
  142.5 10.5 %collective-permute-start.2 = (bf16[1280,128]{1,0:T(8,128)(2,1)}, bf16[1280,128]{1,0:T(8,128)(2,1)}, u32[]{:S(2)}, u32[]{:S(2)}) collective-permute-start(bf16[1280,128]{1,0:T(8,128)(2,1)} %get-tuple-element.264), channel_id=1, source_target_pairs={{0,6},{1,3},{2,4},{3,1},{4,2},{5,7},{6,0},{7,5},{8,14},{9,11},{10,... | collective-permute-start | bytes 983048 | tf_op jit(solution)/shard_map/cond/branch_1_fun/ppermute | solution.py:650
  144.3 9.8 %collective-permute-start.4 = (bf16[1280,128]{1,0:T(8,128)(2,1)}, bf16[1280,128]{1,0:T(8,128)(2,1)S(1)}, u32[]{:S(2)}, u32[]{:S(2)}) collective-permute-start(bf16[1280,128]{1,0:T(8,128)(2,1)} %get-tuple-element.262), channel_id=1, source_target_pairs={{0,24},{1,9},{8,16},{9,1},{16,8},{17,25},{24,0},{25,17},{2,26},{3,... | collective-permute-start | bytes 983048 | tf_op jit(solution)/shard_map/cond/branch_1_fun/ppermute | solution.py:650
  145.1 42.0 %all-to-all-start = ((bf16[8,192,768]{2,1,0:T(8,128)(2,1)}), bf16[8,192,768]{2,1,0:T(8,128)(2,1)S(1)}, u32[]{:S(2)}, u32[]{:S(2)}) async-start(bf16[8,192,768]{2,1,0:T(8,128)(2,1)} %get-tuple-element.64), calls=%async_computation | async-start | bytes 4718592 | tf_op jit(solution)/shard_map/cond/branch_1_fun/all_to_all | solution.py:779
  154.2 7.6 %collective-permute-start.5 = (bf16[2,640,128]{2,1,0:T(8,128)(2,1)S(1)}, bf16[2,640,128]{2,1,0:T(8,128)(2,1)S(1)}, u32[]{:S(2)}, u32[]{:S(2)}) collective-permute-start(bf16[2,640,128]{2,1,0:T(8,128)(2,1)S(1)} %pad_maximum_fusion), channel_id=1, source_target_pairs={{0,32},{1,97},{32,0},{33,65},{64,96},{65,33},{96,64},{97,1},{2,34}... | collective-permute-start | bytes 983048 | tf_op jit(solution)/shard_map/cond/branch_1_fun/ppermute | solution.py:650
  161.9 4.7 %collective-permute-start.6 = (bf16[2,320,128]{2,1,0:T(8,128)(2,1)S(1)}, bf16[2,320,128]{2,1,0:T(8,128)(2,1)S(1)}, u32[]{:S(2)}, u32[]{:S(2)}) collective-permute-start(bf16[2,320,128]{2,1,0:T(8,128)(2,1)S(1)} %get-tuple-element.268), channel_id=1, source_target_pairs={{0,96},{1,33},{32,64},{33,1},{64,32},{65,97},{96,0},{97,65},{2,98}... | collective-permute-start | bytes 491528 | tf_op jit(solution)/shard_map/cond/branch_1_fun/ppermute | solution.py:650
  166.7 5.0 %collective-permute-start.7 = (bf16[320,128]{1,0:T(8,128)(2,1)S(1)}, bf16[320,128]{1,0:T(8,128)(2,1)S(1)}, u32[]{:S(2)}, u32[]{:S(2)}) collective-permute-start(bf16[320,128]{1,0:T(8,128)(2,1)S(1)} %get-tuple-element.273), channel_id=1, source_target_pairs={{0,8},{1,25},{8,0},{9,17},{16,24},{17,9},{24,16},{25,1},{2,10},{3,... | collective-permute-start | bytes 245768 | tf_op jit(solution)/shard_map/cond/branch_1_fun/ppermute | solution.py:650
  167.1 16.6 %collective-permute-start.9 = (bf16[320,128]{1,0:T(8,128)(2,1)S(1)}, bf16[320,128]{1,0:T(8,128)(2,1)S(1)}, u32[]{:S(2)}, u32[]{:S(2)}) collective-permute-start(bf16[320,128]{1,0:T(8,128)(2,1)S(1)} %get-tuple-element.274), channel_id=1, source_target_pairs={{0,2},{1,7},{2,0},{3,5},{4,6},{5,3},{6,4},{7,1},{8,10},{9,15},{10,... | collective-permute-start | bytes 245768 | tf_op jit(solution)/shard_map/cond/branch_1_fun/ppermute | solution.py:650
  171.7 12.1 %collective-permute-start.8 = (bf16[320,128]{1,0:T(8,128)(2,1)S(1)}, bf16[320,128]{1,0:T(8,128)(2,1)S(1)}, u32[]{:S(2)}, u32[]{:S(2)}) collective-permute-start(bf16[320,128]{1,0:T(8,128)(2,1)S(1)} %add_convert_fusion.18), channel_id=1, source_target_pairs={{0,24},{1,9},{8,16},{9,1},{16,8},{17,25},{24,0},{25,17},{2,26},{3,... | collective-permute-start | bytes 245768 | tf_op jit(solution)/shard_map/cond/branch_1_fun/ppermute | solution.py:650
  183.7 3.4 %collective-permute-start.10 = (bf16[320,128]{1,0:T(8,128)(2,1)S(1)}, bf16[320,128]{1,0:T(8,128)(2,1)S(1)}, u32[]{:S(2)}, u32[]{:S(2)}) collective-permute-start(bf16[320,128]{1,0:T(8,128)(2,1)S(1)} %add_convert_fusion.15), channel_id=1, source_target_pairs={{0,6},{1,3},{2,4},{3,1},{4,2},{5,7},{6,0},{7,5},{8,14},{9,11},{10,... | collective-permute-start | bytes 245768 | tf_op jit(solution)/shard_map/cond/branch_1_fun/ppermute | solution.py:650
  187.2 5.6 %collective-permute-start.11 = (bf16[2,320,128]{2,1,0:T(8,128)(2,1)S(1)}, bf16[2,320,128]{2,1,0:T(8,128)(2,1)S(1)}, u32[]{:S(2)}, u32[]{:S(2)}) collective-permute-start(bf16[2,320,128]{2,1,0:T(8,128)(2,1)S(1)} %pad_maximum_fusion.1), channel_id=1, source_target_pairs={{0,96},{1,33},{32,64},{33,1},{64,32},{65,97},{96,0},{97,65},{2,98}... | collective-permute-start | bytes 491528 | tf_op jit(solution)/shard_map/cond/branch_1_fun/ppermute | solution.py:650
  192.8 8.6 %collective-permute-start.12 = (bf16[2,640,128]{2,1,0:T(8,128)(2,1)S(1)}, bf16[2,640,128]{2,1,0:T(8,128)(2,1)S(1)}, u32[]{:S(2)}, u32[]{:S(2)}) collective-permute-start(bf16[2,640,128]{2,1,0:T(8,128)(2,1)S(1)} %maximum_select_fusion.3), channel_id=1, source_target_pairs={{0,32},{1,97},{32,0},{33,65},{64,96},{65,33},{96,64},{97,1},{2,34}... | collective-permute-start | bytes 983048 | tf_op jit(solution)/shard_map/cond/branch_1_fun/ppermute | solution.py:650
  201.7 6.0 %collective-permute-start.14 = (bf16[1280,128]{1,0:T(8,128)(2,1)S(1)}, bf16[1280,128]{1,0:T(8,128)(2,1)S(1)}, u32[]{:S(2)}, u32[]{:S(2)}) collective-permute-start(bf16[1280,128]{1,0:T(8,128)(2,1)S(1)} %get-tuple-element.265), channel_id=1, source_target_pairs={{0,24},{1,9},{8,16},{9,1},{16,8},{17,25},{24,0},{25,17},{2,26},{3,... | collective-permute-start | bytes 983048 | tf_op jit(solution)/shard_map/cond/branch_1_fun/ppermute | solution.py:650
  203.8 6.2 %collective-permute-start.13 = (bf16[1280,128]{1,0:T(8,128)(2,1)S(1)}, bf16[1280,128]{1,0:T(8,128)(2,1)S(1)}, u32[]{:S(2)}, u32[]{:S(2)}) collective-permute-start(bf16[1280,128]{1,0:T(8,128)(2,1)S(1)} %get-tuple-element.266), channel_id=1, source_target_pairs={{0,6},{1,3},{2,4},{3,1},{4,2},{5,7},{6,0},{7,5},{8,14},{9,11},{10,... | collective-permute-start | bytes 983048 | tf_op jit(solution)/shard_map/cond/branch_1_fun/ppermute | solution.py:650
  207.9 15.4 %copy-start.4 = (bf16[2560,128]{1,0:T(8,128)(2,1)}, bf16[2560,128]{1,0:T(8,128)(2,1)S(1)}, u32[]{:S(2)}) copy-start(bf16[2560,128]{1,0:T(8,128)(2,1)S(1)} %maximum_select_fusion.2.refs_1_) | copy-start | bytes 1966084 | tf_op jit(solution)/shard_map/cond
  210.2 13.1 %copy-start.5 = (bf16[2560,128]{1,0:T(8,128)(2,1)}, bf16[2560,128]{1,0:T(8,128)(2,1)S(1)}, u32[]{:S(2)}) copy-start(bf16[2560,128]{1,0:T(8,128)(2,1)S(1)} %maximum_select_fusion.1.refs_0_) | copy-start | bytes 1966084 | tf_op jit(solution)/shard_map/cond
  210.2 13.1 %collective-permute-start.17 = (bf16[2560,128]{1,0:T(8,128)(2,1)S(1)}, bf16[2560,128]{1,0:T(8,128)(2,1)}, u32[]{:S(2)}, u32[]{:S(2)}) collective-permute-start(bf16[2560,128]{1,0:T(8,128)(2,1)S(1)} %maximum_select_fusion.1.refs_0_), channel_id=1, source_target_pairs={{0,1},{1,0},{2,3},{3,2},{4,5},{5,4},{6,7},{7,6},{8,9},{9,8},{10,11... | collective-permute-start | bytes 1966088 | tf_op jit(solution)/shard_map/cond/branch_1_fun/ppermute | solution.py:654
  217.7 5.6 %collective-permute-start.18 = (bf16[2560,128]{1,0:T(8,128)(2,1)S(1)}, bf16[2560,128]{1,0:T(8,128)(2,1)}, u32[]{:S(2)}, u32[]{:S(2)}) collective-permute-start(bf16[2560,128]{1,0:T(8,128)(2,1)S(1)} %maximum_select_fusion.2.refs_1_), channel_id=1, source_target_pairs={{0,1},{1,0},{2,3},{3,2},{4,5},{5,4},{6,7},{7,6},{8,9},{9,8},{10,11... | collective-permute-start | bytes 1966088 | tf_op jit(solution)/shard_map/cond/branch_1_fun/ppermute | solution.py:654
  217.8 18.5 %collective-permute-start.15 = (bf16[2560,128]{1,0:T(8,128)(2,1)S(1)}, bf16[2560,128]{1,0:T(8,128)(2,1)S(1)}, u32[]{:S(2)}, u32[]{:S(2)}) collective-permute-start(bf16[2560,128]{1,0:T(8,128)(2,1)S(1)} %maximum_select_fusion.1.refs_0_), channel_id=1, source_target_pairs={{0,2},{1,7},{2,0},{3,5},{4,6},{5,3},{6,4},{7,1},{8,10},{9,15},{10,... | collective-permute-start | bytes 1966088 | tf_op jit(solution)/shard_map/cond/branch_1_fun/ppermute | solution.py:650
  221.2 17.5 %collective-permute-start.16 = (bf16[2560,128]{1,0:T(8,128)(2,1)S(1)}, bf16[2560,128]{1,0:T(8,128)(2,1)S(1)}, u32[]{:S(2)}, u32[]{:S(2)}) collective-permute-start(bf16[2560,128]{1,0:T(8,128)(2,1)S(1)} %maximum_select_fusion.2.refs_1_), channel_id=1, source_target_pairs={{0,8},{1,25},{8,0},{9,17},{16,24},{17,9},{24,16},{25,1},{2,10},{3,... | collective-permute-start | bytes 1966088 | tf_op jit(solution)/shard_map/cond/branch_1_fun/ppermute | solution.py:650
  236.4 5.6 %copy-start.24 = (bf16[2560,128]{1,0:T(8,128)(2,1)}, bf16[2560,128]{1,0:T(8,128)(2,1)S(1)}, u32[]{:S(2)}) copy-start(bf16[2560,128]{1,0:T(8,128)(2,1)S(1)} %collective-permute-done.15.refs_0_) | copy-start | bytes 1966084 | tf_op jit(solution)/shard_map/cond
  238.7 2.6 collective-permute-start.19
  238.7 3.2 %collective-permute-start.20 = (bf16[2560,128]{1,0:T(8,128)(2,1)S(1)}, bf16[2560,128]{1,0:T(8,128)(2,1)S(1)}, u32[]{:S(2)}, u32[]{:S(2)}) collective-permute-start(bf16[2560,128]{1,0:T(8,128)(2,1)S(1)} %collective-permute-done.16.refs_1_), channel_id=1, source_target_pairs={{0,1},{1,0},{2,3},{3,2},{4,5},{5,4},{6,7},{7,6},{8,9},{9,8},{10,11... | collective-permute-start | bytes 1966088 | tf_op jit(solution)/shard_map/cond/branch_1_fun/ppermute | solution.py:654
  246.9 9.4 %copy-start.7 = (f32[3072]{0:T(1024)}, f32[3072]{0:T(1024)S(1)}, u32[]{:S(2)}) copy-start(f32[3072]{0:T(1024)S(1)} %get-tuple-element.236) | copy-start | bytes 36868
  247.0 9.4 %copy-start.9 = (f32[768]{0:T(1024)}, f32[768]{0:T(1024)S(1)}, u32[]{:S(2)}) copy-start(f32[768]{0:T(1024)S(1)} %get-tuple-element.238) | copy-start | bytes 9220
  247.0 9.4 %copy-start.10 = (f32[768]{0:T(1024)}, f32[768]{0:T(1024)S(1)}, u32[]{:S(2)}) copy-start(f32[768]{0:T(1024)S(1)} %get-tuple-element.240) | copy-start | bytes 9220
  247.0 9.4 %copy-start.11 = (f32[768]{0:T(1024)}, f32[768]{0:T(1024)S(1)}, u32[]{:S(2)}) copy-start(f32[768]{0:T(1024)S(1)} %get-tuple-element.239) | copy-start | bytes 9220
  247.0 9.3 %copy-start.12 = (f32[768]{0:T(1024)}, f32[768]{0:T(1024)S(1)}, u32[]{:S(2)}) copy-start(f32[768]{0:T(1024)S(1)} %get-tuple-element.232) | copy-start | bytes 9220
  247.0 9.3 %copy-start.13 = (f32[768]{0:T(1024)}, f32[768]{0:T(1024)S(1)}, u32[]{:S(2)}) copy-start(f32[768]{0:T(1024)S(1)} %get-tuple-element.234) | copy-start | bytes 9220
  247.0 9.3 %copy-start.1 = (s32[8,512]{1,0:T(8,128)S(1)}, s32[8,512]{1,0:T(8,128)}, u32[]{:S(2)}) copy-start(s32[8,512]{1,0:T(8,128)} %param.26) | copy-start | bytes 49156
  (5 other events, 7.3 us)
Sparse Core Ops, SparseCore 0:
  70.4 173.0 all-reduce.10
